TPU v7x, 32 devices: a whole 2x2x4 slice. The times are simulated.
32 devices in a mesh: mom: 8 (over z, x), tm: 4 (over y, core).
Axes of the slice: x: 2, y: 2, z: 4, core: 2. Of those that a mesh axis runs over, the one named last changes fastest.
Arguments:
- green: bfloat16 [64, 32, 128, 1024], P('mom', None, None, 'tm'), may hold values from -6 to 6
- hole: bfloat16 [64, 32, 128, 1024], P('mom', None, None, 'tm'), may hold values from -6 to 6
- decay_log: float32 [64, 8, 1024], P('mom', None, 'tm'), as said below
- phase_step: float32 [64, 8, 1024], P('mom', None, 'tm'), may hold values from -1 to 1
Outputs:
- collision: bfloat16 [64, 32, 128, 1024], P('mom', None, None, 'tm')
Inputs may be any that keep to these rules, and one draw needn't show every extreme that they name: decay_log holds logarithms of decay factors of at most one.
All inputs are finite; a program needn't handle non-finite values.
Results may differ from a plain program's by a relative error of at most 0.0067.
Values may be sent and summed in bfloat16 or wider, within the bound.
No kernel may reach another device: no remote copies, remote signals or barrier semaphores. Data moves between devices by JAX's collectives and lax.ppermute only.
A program may use at most 256 MiB of HBM per device.

v0:
```python
import math

import jax
import jax.numpy as jnp
from jax import lax
from jax.sharding import PartitionSpec as P

MOMENTA = 64
ORBITALS = 8


step_weight = 0.0625
coupling = 0.25
exact = lax.Precision.HIGHEST


def prefix(x, axis, combine, identity):
    devices, here = (lax.axis_size(axis), lax.axis_index(axis))
    everything = jax.tree.map(lambda part: lax.all_gather(part, axis), x)
    start = jax.tree.map(
        lambda part, zero: jnp.broadcast_to(jnp.asarray(zero, part.dtype), part.shape), x, identity
    )

    def turn(k, before):
        reached = k < here
        new = combine(before, jax.tree.map(lambda part: part[k], everything))
        return jax.tree.map(lambda a, b: jnp.where(reached, a, b), new, before)

    return lax.fori_loop(0, devices, turn, start)


def transform_matrix(handed):
    numbers = jnp.arange(MOMENTA, dtype=jnp.int32)
    product = numbers[:, None] * numbers[None, :] % MOMENTA
    angles = product.astype(jnp.float32) * (2.0 * math.pi / MOMENTA)
    scaled = 1.0 / math.sqrt(MOMENTA)
    cosine = (jnp.cos(angles) * scaled).astype(jnp.bfloat16)
    sine = (handed * jnp.sin(angles) * scaled).astype(jnp.bfloat16)
    upper = jnp.stack([cosine, -sine], axis=-1)
    lower = jnp.stack([sine, cosine], axis=-1)
    return jnp.stack([upper, lower], axis=1)


def transform(matrix, field):
    return jnp.einsum("rokI,kRpIC->rRpoC", matrix, field, preferred_element_type=jnp.float32)


def self_energy(green_space, hole_space):
    green_re = green_space[:, :, :, 0, :]
    green_im = green_space[:, :, :, 1, :]
    hole_re = hole_space[:, :, :, 0, :]
    hole_im = hole_space[:, :, :, 1, :]
    square_re = green_re * green_re - green_im * green_im
    square_im = 2.0 * green_re * green_im
    energy_re = coupling * (square_re * hole_re - square_im * hole_im)
    energy_im = coupling * (square_re * hole_im + square_im * hole_re)
    return jnp.stack([energy_re, energy_im], axis=3).astype(jnp.bfloat16)


def momentum_energy(pieces, plus, minus):
    green_part, hole_part = pieces
    momenta, row_count, field_width, columns = green_part.shape
    layout = (momenta, row_count, field_width // 2, 2, columns)
    green_space = transform(plus, green_part.reshape(layout))
    hole_space = transform(minus, hole_part.reshape(layout))
    sigma_space = self_energy(green_space, hole_space)
    return transform(minus, sigma_space)


def chain_step(earlier, later):
    early_re, early_im, early_hre, early_him = earlier
    later_re, later_im, later_hre, later_him = later
    wide_re = later_re[:, None, None, :]
    wide_im = later_im[:, None, None, :]
    return (
        early_re * later_re - early_im * later_im,
        early_re * later_im + early_im * later_re,
        wide_re * early_hre - wide_im * early_him + later_hre,
        wide_re * early_him + wide_im * early_hre + later_him,
    )


def apply_kernel(signal, kernel):
    return jnp.einsum(
        "kRabs,kbsu->kRabu", signal, kernel, precision=exact, preferred_element_type=jnp.float32
    )


def block_history(packed):
    signal, levels, phases = packed
    columns = signal.shape[-1]
    source_index = lax.broadcasted_iota(jnp.int32, (columns, columns), 0)
    target_index = lax.broadcasted_iota(jnp.int32, (columns, columns), 1)
    causal = target_index >= source_index
    spread = levels[..., None, :] - levels[..., :, None]
    magnitude = jnp.exp(jnp.where(causal, spread, -10000.0))
    twist = phases[..., None, :] - phases[..., :, None]
    kernel_re = magnitude * jnp.cos(twist)
    kernel_im = magnitude * jnp.sin(twist)
    signal_re = signal[..., 0, :]
    signal_im = signal[..., 1, :]
    out_re = apply_kernel(signal_re, kernel_re) - apply_kernel(signal_im, kernel_im)
    out_im = apply_kernel(signal_re, kernel_im) + apply_kernel(signal_im, kernel_re)
    return jnp.stack([out_re, out_im], axis=-2)


def collide(signal, decay_rows, phase_rows):
    momenta = signal.shape[0]
    levels = jnp.cumsum(decay_rows, axis=-1)
    phases = jnp.cumsum(phase_rows, axis=-1)
    blocked = (
        signal.reshape((momenta // momenta, momenta) + signal.shape[1:]),
        levels.reshape((momenta // momenta, momenta) + levels.shape[1:]),
        phases.reshape((momenta // momenta, momenta) + phases.shape[1:]),
    )
    local = lax.map(block_history, blocked).reshape(signal.shape)
    closing = jnp.exp(levels[..., -1])
    product_re = closing * jnp.cos(phases[..., -1])
    product_im = closing * jnp.sin(phases[..., -1])
    ending_re = local[..., 0, -1]
    ending_im = local[..., 1, -1]
    identity = (
        jnp.ones_like(product_re),
        jnp.zeros_like(product_im),
        jnp.zeros_like(ending_re),
        jnp.zeros_like(ending_im),
    )
    incoming = prefix((product_re, product_im, ending_re, ending_im), "tm", chain_step, identity)
    growth = jnp.exp(levels)
    grow_re = (growth * jnp.cos(phases))[:, None, None, :, :]
    grow_im = (growth * jnp.sin(phases))[:, None, None, :, :]
    enter_re = incoming[2][..., None]
    enter_im = incoming[3][..., None]
    added_re = grow_re * enter_re - grow_im * enter_im
    added_im = grow_re * enter_im + grow_im * enter_re
    return step_weight * (local + jnp.stack([added_re, added_im], axis=-2))


def shards(green, hole, decay_log, phase_step):
    plus = transform_matrix(1.0)
    minus = transform_matrix(-1.0)
    energy = momentum_energy(
        (
            lax.all_to_all(green, "mom", split_axis=2, concat_axis=0, tiled=True),
            lax.all_to_all(hole, "mom", split_axis=2, concat_axis=0, tiled=True),
        ),
        plus,
        minus,
    )
    momenta, row_count, pair_width, two_parts, columns = energy.shape
    flat = energy.reshape(momenta, row_count, pair_width * two_parts, columns)
    returned = lax.all_to_all(flat, "mom", split_axis=0, concat_axis=2, tiled=True)
    momenta, row_count, field_width, columns = returned.shape
    grouped = returned.reshape(momenta, row_count, ORBITALS, ORBITALS, 2, columns)
    result = collide(grouped, decay_log, phase_step)
    return result.reshape(momenta, row_count, field_width, columns).astype(jnp.bfloat16)


def solution(mesh):
    in_specs = (
        P("mom", None, None, "tm"),
        P("mom", None, None, "tm"),
        P("mom", None, "tm"),
        P("mom", None, "tm"),
    )
    out_specs = P("mom", None, None, "tm")
    return jax.shard_map(shards, mesh=mesh, in_specs=in_specs, out_specs=out_specs, check_vma=False)
```

profile of v0, /device:TPU:0, one launch (start us, length us, event | category | flops | bytes accessed | tf_op | source)
XLA Modules:
  0.0 2035.3 jit_solution(9625183300139207511)
XLA Ops:
  0.0 16.2 copy.91
  23.5 16.2 copy.89
  39.7 346.8 %all-to-all-done.1 = bf16[8,32,128,256]{3,1,0,2:T(8,128)(2,1)} async-done(((bf16[8,32,128,256]{3,1,0,2:T(8,128)(2,1)}), bf16[8,32,128,256]{3,1,0,2:T(8,128)(2,1)}, u32[]{:S(2)}, u32[]{:S(2)}) %all-to-all-start.1) | async-done | bytes 16777248 | tf_op jit(solution)/shard_map/all_to_all | solution.py:145
  393.3 15.8 copy.92
  409.2 345.7 %all-to-all-done = bf16[8,32,128,256]{3,1,0,2:T(8,128)(2,1)} async-done(((bf16[8,32,128,256]{3,1,0,2:T(8,128)(2,1)}), bf16[8,32,128,256]{3,1,0,2:T(8,128)(2,1)}, u32[]{:S(2)}, u32[]{:S(2)}) %all-to-all-start) | async-done | bytes 16777248 | tf_op jit(solution)/shard_map/all_to_all | solution.py:144
  754.9 15.8 copy.90
  770.7 21.4 %convolution_bitcast_fusion = f32[64,32,8,2,256]{4,0,2,1,3:T(8,128)} fusion(bf16[64,32,8,2,256,1]{4,0,3,2,1,5:T(8,128)(2,1)} %bitcast.150, bf16[64,1,64,2]{2,0,3,1:T(8,128)(2,1)S(1)} %get-tuple-element.259, bf16[64,1,64,2]{2,0,3,1:T(8,128)(2,1)S(1)} %get-tuple-element.260), kind=kOutput, calls=%fused_computation.11 | convolution fusion | flops 2147549184 | bytes 50364416 | tf_op jit(solution)/shard_map/rokI,kRpIC->rRpoC/dot_general | solution.py:45
  792.1 21.4 %convolution_bitcast_fusion.1 = f32[64,32,8,2,256]{4,0,2,1,3:T(8,128)} fusion(bf16[64,32,8,2,256,1]{4,0,3,2,1,5:T(8,128)(2,1)} %bitcast.151, bf16[64,1,64,2]{2,0,3,1:T(8,128)(2,1)S(1)} %get-tuple-element.261, bf16[64,1,64,2]{2,0,3,1:T(8,128)(2,1)S(1)} %get-tuple-element.258), kind=kOutput, calls=%fused_computation.12 | convolution fusion | flops 2147549184 | bytes 50364416 | tf_op jit(solution)/shard_map/rokI,kRpIC->rRpoC/dot_general | solution.py:45
  813.5 29.4 %multiply_convert_fusion.1 = (bf16[64,32,8,1,256]{4,0,2,1,3:T(8,128)(2,1)}, bf16[64,32,8,1,256]{4,0,2,1,3:T(8,128)(2,1)}) fusion(f32[64,32,8,2,256]{4,0,2,1,3:T(8,128)} %convolution_bitcast_fusion, f32[64,32,8,2,256]{4,0,2,1,3:T(8,128)} %convolution_bitcast_fusion.1), kind=kLoop, calls=%fused_computation.27 | loop fusion | flops 62914560 | bytes 83886080 | tf_op jit(solution)/shard_map/convert
  842.9 16.7 fusion.8
  859.6 30.6 %copy.94 = f32[64,32,16,256]{3,2,1,0:T(8,128)} copy(f32[64,32,16,256]{3,0,2,1:T(8,128)} %bitcast.148) | data formatting | bytes 67108864 | tf_op jit(solution)/shard_map/reshape | solution.py:151
  918.6 59.2 %fusion.83 = f32[8,8,256,256,1]{3,2,4,1,0:T(8,128)} fusion(f32[8,8,256]{2,1,0:T(8,128)S(1)} %get-tuple-element.247, f32[8,8,256]{2,1,0:T(8,128)S(1)} %get-tuple-element.246, pred[256,256]{1,0:T(8,128)(4,1)S(1)} %iota_compare_fusion), kind=kLoop, calls=%fused_computation.16.clone.clone.1 | loop fusion | flops 16777216 | bytes 16973824 | tf_op jit(solution)/shard_map/while/body/eval_jaxpr/kRabs,kbsu->kRabu/dot_general | solution.py:84
  977.8 58.9 %fusion.85 = f32[8,8,256,256,1]{3,2,4,1,0:T(8,128)} fusion(f32[8,8,256]{2,1,0:T(8,128)S(1)} %get-tuple-element.247, f32[8,8,256]{2,1,0:T(8,128)S(1)} %get-tuple-element.246, pred[256,256]{1,0:T(8,128)(4,1)S(1)} %iota_compare_fusion), kind=kLoop, calls=%fused_computation.16.clone.1.clone | loop fusion | flops 16777216 | bytes 16973824 | tf_op jit(solution)/shard_map/while/body/eval_jaxpr/kRabs,kbsu->kRabu/dot_general | solution.py:84
  1036.7 581.4 %all-to-all-done.2 = f32[64,32,16,256]{3,2,1,0:T(8,128)} async-done(((f32[64,32,16,256]{3,2,1,0:T(8,128)}), f32[64,32,16,256]{3,2,1,0:T(8,128)}, u32[]{:S(2)}, u32[]{:S(2)}) %all-to-all-start.2) | async-done | bytes 33554464 | tf_op jit(solution)/shard_map/all_to_all | solution.py:152
  1618.1 38.0 %copy.95 = f32[8,32,8,16,256]{4,2,3,1,0:T(8,128)} copy(f32[8,32,8,16,256]{4,3,1,0,2:T(8,128)} %bitcast.39) | data formatting | bytes 67108864 | tf_op jit(solution)/shard_map/all_to_all | solution.py:152
  1656.1 21.5 %fusion.74 = (f32[8,32,8,8,1,256]{5,2,4,3,1,0:T(8,128)}, f32[8,32,8,8,1,256]{5,2,4,3,1,0:T(8,128)}) fusion(f32[8,32,8,8,2,256]{5,2,4,3,1,0:T(8,128)} %bitcast.149), kind=kLoop, calls=%fused_computation.106 | loop fusion | bytes 67108864 | tf_op jit(solution)/shard_map/while/body/eval_jaxpr/slice | solution.py:101
  1677.6 33.5 %fusion.10 = f32[8,8,256,32,8]{2,3,4,1,0:T(8,128)} fusion(f32[8,32,8,8,1,256]{5,2,4,3,1,0:T(8,128)} %get-tuple-element.255, f32[8,8,256,256,1]{3,2,4,1,0:T(8,128)} %fusion.83), kind=kOutput, calls=%fused_computation.31 | convolution fusion | flops 12884901888 | bytes 50331648 | tf_op jit(solution)/shard_map/while/body/eval_jaxpr/kRabs,kbsu->kRabu/dot_general | solution.py:84
  1711.1 89.4 %add_bitcast_fusion = f32[8,32,8,8,1,256]{5,1,2,3,0,4:T(8,128)} fusion(f32[8,8,256,32,8]{2,3,4,1,0:T(8,128)} %fusion.10, f32[8,32,8,8,1,256]{5,2,4,3,1,0:T(8,128)} %get-tuple-element.254, f32[8,8,256]{2,1,0:T(8,128)S(1)} %get-tuple-element.247, f32[8,8,256]{2,1,0:T(8,128)S(1)} %get-tuple-element.246, pred[256,256]{1,0:T(8,128)(4,1)S(1)} %iota_compare_fusion), kind=kOutput, calls=%fused_computation.24 | convolution fusion | flops 12905873408 | bytes 50528256 | tf_op jit(solution)/shard_map/while/body/eval_jaxpr/kRabs,kbsu->kRabu/dot_general | solution.py:84
  1800.5 33.6 %fusion.12 = f32[8,8,256,32,8]{2,3,4,1,0:T(8,128)} fusion(f32[8,32,8,8,1,256]{5,2,4,3,1,0:T(8,128)} %get-tuple-element.254, f32[8,8,256,256,1]{3,2,4,1,0:T(8,128)} %fusion.85), kind=kOutput, calls=%fused_computation.32 | convolution fusion | flops 12884901888 | bytes 50331648 | tf_op jit(solution)/shard_map/while/body/eval_jaxpr/kRabs,kbsu->kRabu/dot_general | solution.py:84
  1834.1 89.0 %subtract_bitcast_fusion = f32[8,32,8,8,1,256]{5,1,2,3,0,4:T(8,128)S(1)} fusion(f32[8,8,256,32,8]{2,3,4,1,0:T(8,128)} %fusion.12, f32[8,32,8,8,1,256]{5,2,4,3,1,0:T(8,128)} %get-tuple-element.255, f32[8,8,256]{2,1,0:T(8,128)S(1)} %get-tuple-element.247, f32[8,8,256]{2,1,0:T(8,128)S(1)} %get-tuple-element.246, pred[256,256]{1,0:T(8,128)(4,1)S(1)} %iota_compare_fusion), kind=kOutput, calls=%fused_computation.25 | convolution fusion | flops 12905873408 | bytes 50528256 | tf_op jit(solution)/shard_map/while/body/eval_jaxpr/kRabs,kbsu->kRabu/dot_general | solution.py:84
  1965.3 10.1 all-gather.3
  1976.7 11.5 multiply_subtract_fusion
  1988.2 27.5 %fusion.3 = bf16[8,32,8,8,2,256]{5,1,2,3,0,4:T(8,128)(2,1)} fusion(f32[8,32,8,8,1,256]{5,1,2,3,0,4:T(8,128)} %add_bitcast_fusion, f32[8,32,8,8,1,256]{5,1,2,3,0,4:T(8,128)} %copy-done, f32[8,32,8,8,1,256]{5,1,2,3,0,4:T(8,128)} %get-tuple-element.257, f32[8,32,8,8,1,256]{5,1,2,3,0,4:T(8,128)} %get-tuple-element.256), kind=kLoop, calls=%fused_computation.8 | loop fusion | flops 41943040 | bytes 83886080 | tf_op jit(solution)/shard_map/convert_element_type | solution.py:156
  2023.9 11.2 copy.111
  (54 shorter events, 94.5 us)
Async XLA Ops:
  16.2 370.3 %all-to-all-start.1 = ((bf16[8,32,128,256]{3,1,0,2:T(8,128)(2,1)}), bf16[8,32,128,256]{3,1,0,2:T(8,128)(2,1)}, u32[]{:S(2)}, u32[]{:S(2)}) async-start(bf16[8,32,128,256]{3,1,0,2:T(8,128)(2,1)} %copy.91), calls=%async_computation.1 | async-start | bytes 33554432 | tf_op jit(solution)/shard_map/all_to_all | solution.py:145
  386.6 368.3 %all-to-all-start = ((bf16[8,32,128,256]{3,1,0,2:T(8,128)(2,1)}), bf16[8,32,128,256]{3,1,0,2:T(8,128)(2,1)}, u32[]{:S(2)}, u32[]{:S(2)}) async-start(bf16[8,32,128,256]{3,1,0,2:T(8,128)(2,1)} %copy.89), calls=%async_computation | async-start | bytes 33554432 | tf_op jit(solution)/shard_map/all_to_all | solution.py:144
  890.2 7.2 copy-start.1
  890.2 12.1 copy-start.2
  890.2 727.9 %all-to-all-start.2 = ((f32[64,32,16,256]{3,2,1,0:T(8,128)}), f32[64,32,16,256]{3,2,1,0:T(8,128)}, u32[]{:S(2)}, u32[]{:S(2)}) async-start(f32[64,32,16,256]{3,2,1,0:T(8,128)} %copy.94), calls=%async_computation.2 | async-start | bytes 67108864 | tf_op jit(solution)/shard_map/all_to_all | solution.py:152
  1923.2 6.2 copy-start
where the time goes:
time: 2040 us
  waiting for transfers between devices  1270 us (62%)
  matrix products  305 us (15%)
  local copies, waits for them, and re-layouts  207 us (10%)
  other arithmetic  197 us (10%)
  blocking collectives  30.6 us (2%)
  starting transfers between devices  20.7 us (1%)
    all_to_all x1, waiting for transfers between devices, shards(): lax.all_to_all(flat, 'mom', split_axis=0, concat_axis=2, tiled=True)  581 us
    all_to_all x1, waiting for transfers between devices, shards(): lax.all_to_all(hole, 'mom', split_axis=2, concat_axis=0, tiled=True)  347 us
    all_to_all x1, waiting for transfers between devices, shards(): lax.all_to_all(green, 'mom', split_axis=2, concat_axis=0, tiled=True)  346 us
    dot_general x4, matrix products, apply_kernel(): jnp.einsum('kRabs,kbsu->kRabu', signal, kernel, precision=exact, preferre...  246 us
    dot_general x2, other arithmetic, apply_kernel(): jnp.einsum('kRabs,kbsu->kRabu', signal, kernel, precision=exact, preferre...  118 us
    dot_general x3, matrix products, transform(): jnp.einsum('rokI,kRpIC->rRpoC', matrix, field, preferred_element_type=jnp...  59.5 us
  transfers between devices with their start and end apart: 3, of which 3 were waited for; matrix products, arithmetic and copies ran while one was open for 8% of the time, Pallas kernels for 0%

commit v1 on v0

v1 whole, which is shorter than its diff:
```python
import functools
import math

import jax
import jax.numpy as jnp
from jax import lax
from jax.experimental import pallas as pl
from jax.experimental.pallas import tpu as pltpu
from jax.sharding import PartitionSpec as P

step_weight = 0.0625
coupling = 0.25
LANES = 128
VMEM = 56 * 1024 * 1024


def shift_columns(x, distance, fill):
    lane = lax.broadcasted_iota(jnp.int32, x.shape, 1)
    return jnp.where(lane >= distance, pltpu.roll(x, distance, 1), fill)


def product(a, b):
    return a[0] * b[0] - a[1] * b[1], a[0] * b[1] + a[1] * b[0]


def prepare_kernel(re_ref, im_ref, step_re, step_im, tile_re, tile_im, full_re, full_im):
    levels = step_re.shape[0]
    carry = None
    for tile in range(re_ref.shape[1] // LANES):
        cut = pl.ds(tile * LANES, LANES)
        base = (re_ref[:, cut], im_ref[:, cut])
        lane = lax.broadcasted_iota(jnp.int32, base[0].shape, 1)
        window = tuple(jnp.where(lane >= 1, part, 0.0) for part in base)
        running = base
        for level in range(levels):
            step_re[level, :, cut] = window[0]
            step_im[level, :, cut] = window[1]
            distance = 1 << level
            window = product(window, tuple(shift_columns(part, distance, 0.0) for part in window))
            running = product(
                running, tuple(shift_columns(part, distance, one) for part, one in zip(running, (1.0, 0.0)))
            )
        tile_re[:, cut] = running[0]
        tile_im[:, cut] = running[1]
        if carry is not None:
            running = product(running, tuple(jnp.broadcast_to(part, running[0].shape) for part in carry))
        full_re[:, cut] = running[0]
        full_im[:, cut] = running[1]
        carry = tuple(part[:, LANES - 1 : LANES] for part in running)


def prepare(lam_re, lam_im):
    rows, columns = lam_re.shape
    levels = int(math.log2(LANES))
    block = min(rows, 64)
    flat = pl.BlockSpec((block, columns), lambda i: (i, 0))
    deep = pl.BlockSpec((levels, block, columns), lambda i: (0, i, 0))
    one = jax.ShapeDtypeStruct((rows, columns), jnp.float32)
    many = jax.ShapeDtypeStruct((levels, rows, columns), jnp.float32)
    return pl.pallas_call(
        prepare_kernel,
        grid=(rows // block,),
        in_specs=[flat, flat],
        out_specs=[deep, deep, flat, flat, flat, flat],
        out_shape=[many, many, one, one, one, one],
        compiler_params=pltpu.CompilerParams(vmem_limit_bytes=VMEM),
        name="prepare",
    )(lam_re, lam_im)


def local_kernel(pieces, plus, minus, back, step_re, step_im, tile_re, tile_im, *refs):
    out_re, out_im, ends, energy, sigma = refs[-5:]
    depth, columns = energy.shape
    half = depth // 2
    levels = step_re.shape[0]
    index = pl.program_id(0) * pl.num_programs(1) + pl.program_id(1)

    def gather(which):
        return pieces[:, which].reshape(depth, columns)

    g = jnp.dot(plus[...], gather(0), preferred_element_type=jnp.float32)
    h = jnp.dot(minus[...], gather(1), preferred_element_type=jnp.float32)
    g_re, g_im, h_re, h_im = g[:half], g[half:], h[:half], h[half:]
    square_re = g_re * g_re - g_im * g_im
    square_im = 2.0 * g_re * g_im
    energy[:half] = (coupling * (square_re * h_re - square_im * h_im)).astype(jnp.bfloat16)
    energy[half:] = (coupling * (square_re * h_im + square_im * h_re)).astype(jnp.bfloat16)
    sigma[...] = jnp.dot(back[...], energy[...], preferred_element_type=jnp.float32)

    carry = None
    for tile in range(columns // LANES):
        cut = pl.ds(tile * LANES, LANES)
        state = (sigma[:half, cut], sigma[half:, cut])
        for level in range(levels):
            moved = tuple(pltpu.roll(part, 1 << level, 1) for part in state)
            added = product((step_re[level, :, cut], step_im[level, :, cut]), moved)
            state = (state[0] + added[0], state[1] + added[1])
        if carry is not None:
            wide = tuple(jnp.broadcast_to(part, state[0].shape) for part in carry)
            added = product((tile_re[:, cut], tile_im[:, cut]), wide)
            state = (state[0] + added[0], state[1] + added[1])
        out_re[0, :, cut] = state[0]
        out_im[0, :, cut] = state[1]
        carry = tuple(part[:, LANES - 1 : LANES] for part in state)
    lane = lax.broadcasted_iota(jnp.int32, (half, LANES), 1)
    for c in range(2):
        ends[c] = jnp.where(lane == index, jnp.broadcast_to(carry[c], (half, LANES)), ends[c])


def local_history(pieces, tables, steps, after):
    parts, _, kl, row_count, width, columns = pieces.shape
    depth = tables[0].shape[0]
    half = depth // 2
    field = depth // (kl * parts)
    grid = (row_count, width // field)
    piece = pl.BlockSpec((parts, 2, kl, 1, field, columns), lambda t, a: (0, 0, 0, t, a, 0))

    def whole(x):
        return pl.BlockSpec(x.shape, lambda t, a: (0,) * x.ndim, pipeline_mode=pl.Buffered(1))

    out = pl.BlockSpec((1, half, columns), lambda t, a: (t * grid[1] + a, 0, 0))
    number = grid[0] * grid[1]
    result = jax.ShapeDtypeStruct((number, half, columns), jnp.float32)
    constants = (*tables, *steps)
    return pl.pallas_call(
        local_kernel,
        grid=grid,
        in_specs=[piece]
        + [whole(x) for x in constants]
        + [pl.BlockSpec(memory_space=pl.ANY)] * len(after),
        out_specs=[out, out, pl.BlockSpec((2, half, LANES), lambda t, a: (0, 0, 0))],
        out_shape=[result, result, jax.ShapeDtypeStruct((2, half, LANES), jnp.float32)],
        scratch_shapes=[pltpu.VMEM((depth, columns), jnp.bfloat16), pltpu.VMEM((depth, columns), jnp.float32)],
        compiler_params=pltpu.CompilerParams(
            dimension_semantics=("arbitrary", "arbitrary"), vmem_limit_bytes=VMEM
        ),
        cost_estimate=pl.CostEstimate(
            flops=number * 30 * depth * depth * columns,
            bytes_accessed=number * depth * columns * 8,
            transcendentals=0,
        ),
        name="local_history",
    )(pieces, *constants, *after)


def finish_kernel(re_ref, im_ref, full_re, full_im, carry, weave, out):
    half, columns = full_re.shape
    index = pl.program_id(0) * pl.num_programs(1) + pl.program_id(1)
    group = weave.shape[0] // 2
    woven = []
    for i in range(half // group):
        rows = pl.ds(i * group, group)
        lane = lax.broadcasted_iota(jnp.int32, (group, LANES), 1)
        enter = tuple(
            jnp.sum(jnp.where(lane == index, carry[c, rows], 0.0), axis=1, keepdims=True) for c in range(2)
        )
        wide = tuple(jnp.broadcast_to(part, (group, columns)) for part in enter)
        added = product((full_re[rows], full_im[rows]), wide)
        both = jnp.concatenate(
            [
                (step_weight * (re_ref[0, rows] + added[0])).astype(jnp.bfloat16),
                (step_weight * (im_ref[0, rows] + added[1])).astype(jnp.bfloat16),
            ],
            axis=0,
        )
        woven.append(jnp.dot(weave[...], both, preferred_element_type=jnp.float32).astype(jnp.bfloat16))
    out[...] = jnp.concatenate(woven, axis=0).reshape(out.shape)


def finish(parts, momenta, local_re, local_im, full_re, full_im, carry, weave, grid):
    half, columns = full_re.shape
    field = 2 * half // momenta
    kl = momenta // parts
    step = pl.BlockSpec((1, half, columns), lambda t, a: (t * grid[1] + a, 0, 0))

    def whole(x):
        return pl.BlockSpec(x.shape, lambda t, a: (0,) * x.ndim, pipeline_mode=pl.Buffered(1))

    piece = pl.BlockSpec((parts, kl, 1, field, columns), lambda t, a: (0, 0, t, a, 0))
    return pl.pallas_call(
        finish_kernel,
        grid=grid,
        in_specs=[step, step, whole(full_re), whole(full_im), whole(carry), whole(weave)],
        out_specs=piece,
        out_shape=jax.ShapeDtypeStruct((parts, kl, grid[0], grid[1] * field, columns), jnp.bfloat16),
        compiler_params=pltpu.CompilerParams(
            dimension_semantics=("arbitrary", "arbitrary"), vmem_limit_bytes=VMEM
        ),
        cost_estimate=pl.CostEstimate(
            flops=grid[0] * grid[1] * half * columns * 10,
            bytes_accessed=grid[0] * grid[1] * half * columns * 30,
            transcendentals=0,
        ),
        name="finish",
    )(local_re, local_im, full_re, full_im, carry, weave)


def pack_kernel(green, hole, *refs):
    out = refs[-1]
    out[0, 0] = green[...]
    out[0, 1] = hole[...]


def pack(green, hole, parts, start, wide, after):
    kl, row_count, _, columns = green.shape
    share = row_count // parts
    steps = math.gcd(kl, 2)
    block = (kl // steps, share, wide, columns)
    inward = pl.BlockSpec(block, lambda j, i: (i, j, start // wide, 0))
    shape = (parts, 2, kl, share, wide, columns)
    return pl.pallas_call(
        pack_kernel,
        grid=(parts, steps),
        in_specs=[inward, inward] + [pl.BlockSpec(memory_space=pl.ANY)] * len(after),
        out_specs=pl.BlockSpec((1, 2, *block), lambda j, i: (j, 0, i, 0, 0, 0)),
        out_shape=jax.ShapeDtypeStruct(shape, green.dtype),
        compiler_params=pltpu.CompilerParams(vmem_limit_bytes=VMEM),
        cost_estimate=pl.CostEstimate(flops=0, bytes_accessed=4 * math.prod(shape), transcendentals=0),
        name="pack",
    )(green, hole, *after)


def place_kernel(pieces, *refs):
    refs[-1][...] = pieces[0]


def place(result, pieces, start, shape):
    parts, kl, share, wide, columns = pieces.shape
    held = [] if result is None else [result]
    steps = math.gcd(kl, 2)
    block = (kl // steps, share, wide, columns)
    return pl.pallas_call(
        place_kernel,
        grid=(parts, steps),
        in_specs=[pl.BlockSpec((1, *block), lambda j, i: (j, i, 0, 0, 0))]
        + [pl.BlockSpec(memory_space=pl.ANY)] * len(held),
        out_specs=pl.BlockSpec(block, lambda j, i: (i, j, start // wide, 0)),
        out_shape=jax.ShapeDtypeStruct(shape, pieces.dtype),
        input_output_aliases={1: 0} if held else {},
        compiler_params=pltpu.CompilerParams(vmem_limit_bytes=VMEM),
        cost_estimate=pl.CostEstimate(flops=0, bytes_accessed=4 * math.prod(pieces.shape), transcendentals=0),
        name="place",
    )(pieces, *held)


def entry(momenta, handed, site, out_part, momentum, in_part):
    angle = (site * momentum % momenta).astype(jnp.float32) * (2.0 * math.pi / momenta)
    scaled = 1.0 / math.sqrt(momenta)
    cosine = (jnp.cos(angle) * scaled).astype(jnp.bfloat16)
    sine = (handed * jnp.sin(angle) * scaled).astype(jnp.bfloat16)
    return jnp.where(out_part == in_part, cosine, jnp.where(out_part == 0, -sine, sine))


def transform_tables(momenta, orbitals, order):
    depth = momenta * orbitals * 2
    major = jnp.arange(depth, dtype=jnp.int32)
    field_k = jnp.repeat(order, orbitals * 2)
    field_b = major // 2 % orbitals
    field_c = major % 2
    inner_c = major // (momenta * orbitals)
    inner_r = major // orbitals % momenta
    inner_b = major % orbitals
    inner_k = jnp.tile(jnp.repeat(order, orbitals), 2)

    def table(handed, rows, cols):
        (r, b, o), (k, d, i) = (tuple(x[:, None] for x in rows), tuple(x[None, :] for x in cols))
        value = entry(momenta, handed, r, o, k, i)
        return jnp.where(b == d, value, jnp.zeros_like(value))

    inner = (inner_r, inner_b, inner_c)
    plus = table(1.0, inner, (field_k, field_b, field_c))
    minus = table(-1.0, inner, (field_k, field_b, field_c))
    back = table(-1.0, (inner_k, inner_b, inner_c), inner)
    return plus, minus, back


def weave_table(group):
    row = lax.broadcasted_iota(jnp.int32, (2 * group, 2 * group), 0)
    col = lax.broadcasted_iota(jnp.int32, (2 * group, 2 * group), 1)
    return (col == row // 2 + group * (row % 2)).astype(jnp.bfloat16)


def carries(axis, ends, total_re, total_im):
    devices, here = lax.axis_size(axis), lax.axis_index(axis)
    flat = jnp.swapaxes(ends, 1, 2)
    everything = lax.all_gather(flat, axis)
    state = (jnp.zeros_like(flat[0]), jnp.zeros_like(flat[1]))
    for k in range(devices - 1):
        moved = product((total_re[k][None, :], total_im[k][None, :]), state)
        new = (moved[0] + everything[k, 0], moved[1] + everything[k, 1])
        state = tuple(jnp.where(k < here, a, b) for a, b in zip(new, state))
    return jnp.swapaxes(jnp.stack(state), 1, 2)


def shards(green, hole, decay_log, phase_step):
    parts, here = lax.axis_size("mom"), lax.axis_index("mom")
    kl, row_count, width, columns = green.shape
    orbitals = decay_log.shape[1]
    momenta = kl * parts
    field = 2 * orbitals
    share = row_count // parts
    pairs = width // field
    sizes = [pairs // 2] * 2 if parts <= pairs else [pairs]
    starts = [sum(sizes[:i]) * field for i in range(len(sizes))]

    both = lax.all_gather(jnp.stack([decay_log, phase_step]), "mom", axis=1, tiled=True)
    damp, turn = (x.reshape(momenta * orbitals, columns) for x in both)
    decay = jnp.exp(damp)
    step_re, step_im, tile_re, tile_im, full_re, full_im = prepare(decay * jnp.cos(turn), decay * jnp.sin(turn))
    totals = lax.all_gather(jnp.stack([full_re[:, -1], full_im[:, -1]]), "tm")
    tables = transform_tables(momenta, orbitals, jnp.arange(momenta, dtype=jnp.int32))
    group = min(momenta, 8) * orbitals
    weave = weave_table(group)

    def exchange(x):
        return lax.all_to_all(x, "mom", split_axis=0, concat_axis=0, tiled=True)

    arrived = [
        exchange(pack(green, hole, parts, start, size * field, [both] if start == 0 else []))
        for start, size in zip(starts, sizes)
    ]
    result, after = None, []
    for pieces, start, size in zip(arrived, starts, sizes):
        local_re, local_im, ends = local_history(pieces, tables, (step_re, step_im, tile_re, tile_im), after)
        number = share * size
        enter = carries("tm", ends[:, :, :number], totals[:, 0], totals[:, 1])
        enter = jnp.pad(enter, ((0, 0), (0, 0), (0, LANES - number)))
        pieces = finish(parts, momenta, local_re, local_im, full_re, full_im, enter, weave, (share, size))
        after = [pieces]
        result = place(result, exchange(pieces), start, green.shape)
    return result


def solution(mesh):
    in_specs = (
        P("mom", None, None, "tm"),
        P("mom", None, None, "tm"),
        P("mom", None, "tm"),
        P("mom", None, "tm"),
    )
    out_specs = P("mom", None, None, "tm")
    return jax.shard_map(shards, mesh=mesh, in_specs=in_specs, out_specs=out_specs, check_vma=False)
```

time: 2040 us -> 1200 us (0.59)
  waiting for transfers between devices: 1270 us -> 821 us
  matrix products: 305 us -> 0 us
  Pallas kernels: 0 us -> 275 us
  local copies, waits for them, and re-layouts: 207 us -> 6.25 us
  other arithmetic: 197 us -> 44 us
    all_to_all x3 -> x4, waiting for transfers between devices: 1270 us -> 776 us  [exchange(): return lax.all_to_all(x, 'mom', split_axis=0, concat_axis=0, tiled=True)]
    dot_general x7 -> x0, matrix products: 305 us -> none  [the longest x4 246 us: apply_kernel(): jnp.einsum('kRabs,kbsu->kRabu', signal, kernel, precision=exact, preferre...]
    pallas_call x0 -> x9, Pallas kernels: none -> 275 us  [the longest x2 172 us: local_history(): pl.pallas_call(local_kernel, grid=grid, in_specs=[piece] + [whole(x) for...]
    dot_general x2 -> x0, other arithmetic: 118 us -> none  [apply_kernel(): jnp.einsum('kRabs,kbsu->kRabu', signal, kernel, precision=exact, preferre...]
    all_to_all x3 -> x0, local copies, waits for them, and re-layouts: 69.6 us -> none  [the longest x1 38 us: shards(): lax.all_to_all(flat, 'mom', split_axis=0, concat_axis=2, tiled=True)]
    slice x7 -> x1, local copies, waits for them, and re-layouts: 47.5 us -> 1.4 us  [shards(): totals = lax.all_gather(jnp.stack([full_re[:, -1], full_im[:, -1]]), 'tm')]
    all_gather x0 -> x1, waiting for transfers between devices: none -> 44.4 us  [shards(): lax.all_gather(jnp.stack([decay_log, phase_step]), 'mom', axis=1, tiled=T...]
    unnamed x10 -> x4, local copies, waits for them, and re-layouts: 38.9 us -> 0.01 us
  transfers between devices with their start and end apart: 3 -> 5, of which waited for: 3 -> 5; matrix products, arithmetic and copies ran while one was open for 8% -> 4% of each run, Pallas kernels for 0% -> 21%
where the time goes in v1:
time: 1200 us
  waiting for transfers between devices  821 us (68%)
  Pallas kernels  275 us (23%)
  other arithmetic  44 us (4%)
  starting transfers between devices  21.6 us (2%)
  blocking collectives  17 us (1%)
  between operations  13.6 us (1%)
    all_to_all x4, waiting for transfers between devices, exchange(): return lax.all_to_all(x, 'mom', split_axis=0, concat_axis=0, tiled=True)  776 us
    pallas_call x2, Pallas kernels, local_history(): pl.pallas_call(local_kernel, grid=grid, in_specs=[piece] + [whole(x) for...  172 us
    all_gather x1, waiting for transfers between devices, shards(): lax.all_gather(jnp.stack([decay_log, phase_step]), 'mom', axis=1, tiled=T...  44.4 us
    select_n x1, other arithmetic, table(): return jnp.where(b == d, value, jnp.zeros_like(value))  38.8 us
    pallas_call x2, Pallas kernels, pack(): pl.pallas_call(pack_kernel, grid=(parts, steps), in_specs=[inward, inward...  34.5 us
    pallas_call x2, Pallas kernels, finish(): pl.pallas_call(finish_kernel, grid=grid, in_specs=[step, step, whole(full...  34.3 us
  transfers between devices with their start and end apart: 5, of which 5 were waited for; matrix products, arithmetic and copies ran while one was open for 4% of the time, Pallas kernels for 21%

profile of v1, /device:TPU:0, one launch (start us, length us, event | category | flops | bytes accessed | tf_op | source)
XLA Modules:
  0.0 1198.2 jit_solution(10065854174709423761)
XLA Ops:
  6.5 1.5 pad_maximum_fusion
  8.1 44.4 %all-gather.6.cloned.1.call-done.refs_0_ = f32[2,64,8,256]{3,2,1,0:T(8,128)} async-done(((f32[2,8,8,256]{3,2,1,0:T(8,128)}), f32[2,64,8,256]{3,2,1,0:T(8,128)}) %all-gather.6.cloned.1.call-update) | async-done | bytes 1048592 | tf_op jit(solution)/shard_map/all_gather | solution.py:306
  52.5 17.3 %pack.3 = bf16[8,2,8,4,64,256]{5,4,3,2,1,0:T(8,128)(2,1)} custom-call(bf16[8,32,128,256]{3,2,1,0:T(8,128)(2,1)} %green.3, bf16[8,32,128,256]{3,2,1,0:T(8,128)(2,1)} %hole.3, f32[2,64,8,256]{3,2,1,0:T(8,128)} %all-gather.6.cloned.1.call-done.refs_0_), custom_call_target="tpu_custom_call" | custom-call | bytes 33554432 | tf_op jit(solution)/shard_map/pack/pallas_call | solution.py:211
  69.7 5.7 all-to-all-start.1
  75.5 17.3 %pack.2 = bf16[8,2,8,4,64,256]{5,4,3,2,1,0:T(8,128)(2,1)} custom-call(bf16[8,32,128,256]{3,2,1,0:T(8,128)(2,1)} %green.3, bf16[8,32,128,256]{3,2,1,0:T(8,128)(2,1)} %hole.3), custom_call_target="tpu_custom_call" | custom-call | bytes 33554432 | tf_op jit(solution)/shard_map/pack/pallas_call | solution.py:211
  92.8 344.8 %all-to-all-done.1.pieces = bf16[8,2,8,4,64,256]{5,4,3,2,1,0:T(8,128)(2,1)} async-done(((bf16[8,2,8,4,64,256]{5,4,3,2,1,0:T(8,128)(2,1)}), bf16[8,2,8,4,64,256]{5,4,3,2,1,0:T(8,128)(2,1)}, u32[]{:S(2)}, u32[]{:S(2)}) %all-to-all-start.1) | async-done | bytes 16777248 | tf_op jit(solution)/shard_map/all_to_all | solution.py:316
  437.6 5.7 all-to-all-start
  444.4 38.8 %compare_select_fusion.2 = (bf16[1024,1024]{1,0:T(8,128)(2,1)}, bf16[1024,1024]{1,0:T(8,128)(2,1)}, bf16[1024,1024]{1,0:T(8,128)(2,1)}) fusion(s32[1024]{0:T(1024)S(1)} %mul.437, s32[1024]{0:T(1024)S(1)} %get-tuple-element.47, s32[1024]{0:T(1024)S(1)} %get-tuple-element.46, s32[1024]{0:T(1024)S(1)} %get-tuple-element.49, s32[1024]{0:T(1024)S(1)} %get-tuple-element.48, ...), kind=kLoop, calls=%fused_computation.12 | loop fusion | flops 62914560 | bytes 6321152 | tf_op jit(solution)/shard_map/jit(_where)/select_n | solution.py:268
  483.2 2.7 multiply_bitcast_fusion
  485.9 10.1 prepare.1
  497.4 5.4 all-gather.3
  502.8 86.2 %local_history.2 = (f32[16,512,256]{2,1,0:T(8,128)}, f32[16,512,256]{2,1,0:T(8,128)}, f32[2,512,128]{2,1,0:T(8,128)}) custom-call(bf16[8,2,8,4,64,256]{5,4,3,2,1,0:T(8,128)(2,1)} %all-to-all-done.1.pieces, bf16[1024,1024]{1,0:T(8,128)(2,1)} %get-tuple-element.38.plus, bf16[1024,1024]{1,0:T(8,128)(2,1)} %get-tuple-element.37.minus, ...), custom_call_target="tpu_custom_call" | custom-call | flops 128849018880 | bytes 33554432 | tf_op jit(solution)/shard_map/local_history/pallas_call | solution.py:125
  590.2 5.8 all-gather.1
  597.2 17.2 %finish.2.refs_0_ = bf16[8,8,4,64,256]{4,3,2,1,0:T(8,128)(2,1)} custom-call(f32[16,512,256]{2,1,0:T(8,128)} %get-tuple-element.21.re_ref, f32[16,512,256]{2,1,0:T(8,128)} %get-tuple-element.22.im_ref, f32[512,256]{1,0:T(8,128)} %get-tuple-element.23.full_re, f32[512,256]{1,0:T(8,128)} %get-tuple-element.24.full_im, f32[2,512,128]{2,1,0:T(8,128)} %pad.7.carry, ...), custom_call_target="tpu_custom_call" | custom-call | flops 20971520 | bytes 62914560 | tf_op jit(solution)/shard_map/finish/pallas_call | solution.py:180
  614.4 190.2 %all-to-all-done.pieces = bf16[8,2,8,4,64,256]{5,4,3,2,1,0:T(8,128)(2,1)} async-done(((bf16[8,2,8,4,64,256]{5,4,3,2,1,0:T(8,128)(2,1)}), bf16[8,2,8,4,64,256]{5,4,3,2,1,0:T(8,128)(2,1)}, u32[]{:S(2)}, u32[]{:S(2)}) %all-to-all-start) | async-done | bytes 16777248 | tf_op jit(solution)/shard_map/all_to_all | solution.py:316
  804.6 5.0 all-to-all-start.3
  809.6 86.1 %local_history.3 = (f32[16,512,256]{2,1,0:T(8,128)}, f32[16,512,256]{2,1,0:T(8,128)}, f32[2,512,128]{2,1,0:T(8,128)}) custom-call(bf16[8,2,8,4,64,256]{5,4,3,2,1,0:T(8,128)(2,1)} %all-to-all-done.pieces, bf16[1024,1024]{1,0:T(8,128)(2,1)} %get-tuple-element.38.plus, bf16[1024,1024]{1,0:T(8,128)(2,1)} %get-tuple-element.37.minus, ...), custom_call_target="tpu_custom_call" | custom-call | flops 128849018880 | bytes 33554432 | tf_op jit(solution)/shard_map/local_history/pallas_call | solution.py:125
  897.0 5.8 all-gather.2
  903.9 17.1 %finish.3 = bf16[8,8,4,64,256]{4,3,2,1,0:T(8,128)(2,1)} custom-call(f32[16,512,256]{2,1,0:T(8,128)} %get-tuple-element.26.re_ref, f32[16,512,256]{2,1,0:T(8,128)} %get-tuple-element.27.im_ref, f32[512,256]{1,0:T(8,128)} %get-tuple-element.23.full_re, f32[512,256]{1,0:T(8,128)} %get-tuple-element.24.full_im, f32[2,512,128]{2,1,0:T(8,128)} %pad.8.carry, ...), custom_call_target="tpu_custom_call" | custom-call | flops 20971520 | bytes 62914560 | tf_op jit(solution)/shard_map/finish/pallas_call | solution.py:180
  921.1 71.2 %all-to-all-done.3.pieces = bf16[8,8,4,64,256]{4,3,2,1,0:T(8,128)(2,1)} async-done(((bf16[8,8,4,64,256]{4,3,2,1,0:T(8,128)(2,1)}), bf16[8,8,4,64,256]{4,3,2,1,0:T(8,128)(2,1)}, u32[]{:S(2)}, u32[]{:S(2)}) %all-to-all-start.3) | async-done | bytes 8388640 | tf_op jit(solution)/shard_map/all_to_all | solution.py:316
  992.3 5.0 all-to-all-start.2
  997.3 11.9 place.2.refs_0_
  1009.2 170.2 %all-to-all-done.2.pieces = bf16[8,8,4,64,256]{4,3,2,1,0:T(8,128)(2,1)} async-done(((bf16[8,8,4,64,256]{4,3,2,1,0:T(8,128)(2,1)}), bf16[8,8,4,64,256]{4,3,2,1,0:T(8,128)(2,1)}, u32[]{:S(2)}, u32[]{:S(2)}) %all-to-all-start.2) | async-done | bytes 8388640 | tf_op jit(solution)/shard_map/all_to_all | solution.py:316
  1179.5 11.9 place.3
  (35 shorter events, 7.2 us)
Async XLA Ops:
  6.5 45.9 %all-gather.6.cloned.1.call-start = ((), (), s32[]{:S(2)}) async-start(), calls=%async_computation.4 | async-start | bytes 1179648 | tf_op jit(solution)/shard_map/all_gather | solution.py:306
  69.7 367.9 %all-to-all-start.1 = ((bf16[8,2,8,4,64,256]{5,4,3,2,1,0:T(8,128)(2,1)}), bf16[8,2,8,4,64,256]{5,4,3,2,1,0:T(8,128)(2,1)}, u32[]{:S(2)}, u32[]{:S(2)}) async-start(bf16[8,2,8,4,64,256]{5,4,3,2,1,0:T(8,128)(2,1)} %pack.3), calls=%async_computation.1 | async-start | bytes 33554432 | tf_op jit(solution)/shard_map/all_to_all | solution.py:316
  437.6 367.0 %all-to-all-start = ((bf16[8,2,8,4,64,256]{5,4,3,2,1,0:T(8,128)(2,1)}), bf16[8,2,8,4,64,256]{5,4,3,2,1,0:T(8,128)(2,1)}, u32[]{:S(2)}, u32[]{:S(2)}) async-start(bf16[8,2,8,4,64,256]{5,4,3,2,1,0:T(8,128)(2,1)} %pack.2), calls=%async_computation | async-start | bytes 33554432 | tf_op jit(solution)/shard_map/all_to_all | solution.py:316
  443.3 39.9 %copy-start = (f32[2,64,8,256]{3,2,1,0:T(8,128)S(1)}, f32[2,64,8,256]{3,2,1,0:T(8,128)}, u32[]{:S(2)}) copy-start(f32[2,64,8,256]{3,2,1,0:T(8,128)} %all-gather.6.cloned.1.call-done.refs_0_) | copy-start | bytes 3145732
  804.6 187.7 %all-to-all-start.3 = ((bf16[8,8,4,64,256]{4,3,2,1,0:T(8,128)(2,1)}), bf16[8,8,4,64,256]{4,3,2,1,0:T(8,128)(2,1)}, u32[]{:S(2)}, u32[]{:S(2)}) async-start(bf16[8,8,4,64,256]{4,3,2,1,0:T(8,128)(2,1)} %finish.2.refs_0_), calls=%async_computation.3 | async-start | bytes 16777216 | tf_op jit(solution)/shard_map/all_to_all | solution.py:316
  992.3 187.2 %all-to-all-start.2 = ((bf16[8,8,4,64,256]{4,3,2,1,0:T(8,128)(2,1)}), bf16[8,8,4,64,256]{4,3,2,1,0:T(8,128)(2,1)}, u32[]{:S(2)}, u32[]{:S(2)}) async-start(bf16[8,8,4,64,256]{4,3,2,1,0:T(8,128)(2,1)} %finish.3), calls=%async_computation.2 | async-start | bytes 16777216 | tf_op jit(solution)/shard_map/all_to_all | solution.py:316
Sparse Core Ops, SparseCore 0:
  9.5 42.8 all-gather.5

commit v2 on v1

--- a/solution.py
+++ b/solution.py
@@ -23,7 +23,7 @@
     return a[0] * b[0] - a[1] * b[1], a[0] * b[1] + a[1] * b[0]
 
 
-def prepare_kernel(re_ref, im_ref, step_re, step_im, tile_re, tile_im, full_re, full_im):
+def prepare_kernel(_, re_ref, im_ref, step_re, step_im, tile_re, tile_im, full_re, full_im):
     levels = step_re.shape[0]
     carry = None
     for tile in range(re_ref.shape[1] // LANES):
@@ -49,34 +49,45 @@
         carry = tuple(part[:, LANES - 1 : LANES] for part in running)
 
 
-def prepare(lam_re, lam_im):
+def prepare(positions, lam_re, lam_im):
     rows, columns = lam_re.shape
     levels = int(math.log2(LANES))
-    block = min(rows, 64)
-    flat = pl.BlockSpec((block, columns), lambda i: (i, 0))
-    deep = pl.BlockSpec((levels, block, columns), lambda i: (0, i, 0))
+    block = rows // positions.shape[0]
+    inward = pl.BlockSpec((block, columns), lambda i, positions: (positions[i], 0))
+    flat = pl.BlockSpec((block, columns), lambda i, positions: (i, 0))
+    deep = pl.BlockSpec((levels, block, columns), lambda i, positions: (0, i, 0))
     one = jax.ShapeDtypeStruct((rows, columns), jnp.float32)
     many = jax.ShapeDtypeStruct((levels, rows, columns), jnp.float32)
     return pl.pallas_call(
         prepare_kernel,
-        grid=(rows // block,),
-        in_specs=[flat, flat],
-        out_specs=[deep, deep, flat, flat, flat, flat],
+        grid_spec=pltpu.PrefetchScalarGridSpec(
+            num_scalar_prefetch=1,
+            grid=(rows // block,),
+            in_specs=[inward, inward],
+            out_specs=[deep, deep, flat, flat, flat, flat],
+        ),
         out_shape=[many, many, one, one, one, one],
         compiler_params=pltpu.CompilerParams(vmem_limit_bytes=VMEM),
         name="prepare",
-    )(lam_re, lam_im)
-
-
-def local_kernel(pieces, plus, minus, back, step_re, step_im, tile_re, tile_im, *refs):
-    out_re, out_im, ends, energy, sigma = refs[-5:]
+    )(positions, lam_re, lam_im)
+
+
+def local_kernel(count, partner, *refs):
+    pieces, constants, (out_re, out_im, ends, energy, sigma, field) = refs[:count], refs[count : count + 7], refs[-6:]
+    plus, minus, back, step_re, step_im, tile_re, tile_im = constants
     depth, columns = energy.shape
     half = depth // 2
     levels = step_re.shape[0]
     index = pl.program_id(0) * pl.num_programs(1) + pl.program_id(1)
 
+    if count == 1:
+        field = pieces[0]
+    else:
+        for j, piece in enumerate(pieces):
+            field[partner[j]] = piece[...]
+
     def gather(which):
-        return pieces[:, which].reshape(depth, columns)
+        return field[:, which].reshape(depth, columns)
 
     g = jnp.dot(plus[...], gather(0), preferred_element_type=jnp.float32)
     h = jnp.dot(minus[...], gather(1), preferred_element_type=jnp.float32)
@@ -107,30 +118,40 @@
         ends[c] = jnp.where(lane == index, jnp.broadcast_to(carry[c], (half, LANES)), ends[c])
 
 
-def local_history(pieces, tables, steps, after):
-    parts, _, kl, row_count, width, columns = pieces.shape
+def local_history(pieces, partner, tables, steps, after):
+    parts = partner.shape[0]
+    kl, row_count, width, columns = pieces[0].shape[-4:]
     depth = tables[0].shape[0]
     half = depth // 2
     field = depth // (kl * parts)
     grid = (row_count, width // field)
-    piece = pl.BlockSpec((parts, 2, kl, 1, field, columns), lambda t, a: (0, 0, 0, t, a, 0))
+    lead = pieces[0].ndim - 5
+    block = (2, kl, 1, field, columns)
+    piece = pl.BlockSpec((parts,) * lead + block, lambda t, a, p: (0,) * (lead + 2) + (t, a, 0))
 
     def whole(x):
-        return pl.BlockSpec(x.shape, lambda t, a: (0,) * x.ndim, pipeline_mode=pl.Buffered(1))
-
-    out = pl.BlockSpec((1, half, columns), lambda t, a: (t * grid[1] + a, 0, 0))
+        return pl.BlockSpec(x.shape, lambda t, a, p: (0,) * x.ndim, pipeline_mode=pl.Buffered(1))
+
+    out = pl.BlockSpec((1, half, columns), lambda t, a, p: (t * grid[1] + a, 0, 0))
     number = grid[0] * grid[1]
     result = jax.ShapeDtypeStruct((number, half, columns), jnp.float32)
     constants = (*tables, *steps)
     return pl.pallas_call(
-        local_kernel,
-        grid=grid,
-        in_specs=[piece]
-        + [whole(x) for x in constants]
-        + [pl.BlockSpec(memory_space=pl.ANY)] * len(after),
-        out_specs=[out, out, pl.BlockSpec((2, half, LANES), lambda t, a: (0, 0, 0))],
+        functools.partial(local_kernel, len(pieces)),
+        grid_spec=pltpu.PrefetchScalarGridSpec(
+            num_scalar_prefetch=1,
+            grid=grid,
+            in_specs=[piece] * len(pieces)
+            + [whole(x) for x in constants]
+            + [pl.BlockSpec(memory_space=pl.ANY)] * len(after),
+            out_specs=[out, out, pl.BlockSpec((2, half, LANES), lambda t, a, p: (0, 0, 0))],
+            scratch_shapes=[
+                pltpu.VMEM((depth, columns), jnp.bfloat16),
+                pltpu.VMEM((depth, columns), jnp.float32),
+                pltpu.VMEM((parts, *block), jnp.bfloat16),
+            ],
+        ),
         out_shape=[result, result, jax.ShapeDtypeStruct((2, half, LANES), jnp.float32)],
-        scratch_shapes=[pltpu.VMEM((depth, columns), jnp.bfloat16), pltpu.VMEM((depth, columns), jnp.float32)],
         compiler_params=pltpu.CompilerParams(
             dimension_semantics=("arbitrary", "arbitrary"), vmem_limit_bytes=VMEM
         ),
@@ -140,10 +161,11 @@
             transcendentals=0,
         ),
         name="local_history",
-    )(pieces, *constants, *after)
-
-
-def finish_kernel(re_ref, im_ref, full_re, full_im, carry, weave, out):
+    )(partner, *pieces, *constants, *after)
+
+
+def finish_kernel(count, partner, re_ref, im_ref, full_re, full_im, carry, weave, *refs):
+    outs, hold = refs[-1 - count : -1], refs[-1]
     half, columns = full_re.shape
     index = pl.program_id(0) * pl.num_programs(1) + pl.program_id(1)
     group = weave.shape[0] // 2
@@ -164,25 +186,41 @@
             axis=0,
         )
         woven.append(jnp.dot(weave[...], both, preferred_element_type=jnp.float32).astype(jnp.bfloat16))
-    out[...] = jnp.concatenate(woven, axis=0).reshape(out.shape)
-
-
-def finish(parts, momenta, local_re, local_im, full_re, full_im, carry, weave, grid):
+    if count == 1:
+        outs[0][...] = jnp.concatenate(woven, axis=0).reshape(outs[0].shape)
+    else:
+        hold[...] = jnp.concatenate(woven, axis=0).reshape(hold.shape)
+        for j, out in enumerate(outs):
+            out[...] = hold[partner[j]]
+
+
+def finish(held, offset, total, partner, split, momenta, local_re, local_im, full_re, full_im, carry, weave, grid):
+    parts = partner.shape[0]
     half, columns = full_re.shape
     field = 2 * half // momenta
     kl = momenta // parts
-    step = pl.BlockSpec((1, half, columns), lambda t, a: (t * grid[1] + a, 0, 0))
+    step = pl.BlockSpec((1, half, columns), lambda t, a, p: (t * grid[1] + a, 0, 0))
 
     def whole(x):
-        return pl.BlockSpec(x.shape, lambda t, a: (0,) * x.ndim, pipeline_mode=pl.Buffered(1))
-
-    piece = pl.BlockSpec((parts, kl, 1, field, columns), lambda t, a: (0, 0, t, a, 0))
-    return pl.pallas_call(
-        finish_kernel,
-        grid=grid,
-        in_specs=[step, step, whole(full_re), whole(full_im), whole(carry), whole(weave)],
-        out_specs=piece,
-        out_shape=jax.ShapeDtypeStruct((parts, kl, grid[0], grid[1] * field, columns), jnp.bfloat16),
+        return pl.BlockSpec(x.shape, lambda t, a, p: (0,) * x.ndim, pipeline_mode=pl.Buffered(1))
+
+    held = [] if held is None else [held]
+    lead = () if split else (parts,)
+    block = (kl, 1, field, columns)
+    count = parts if split else 1
+    return pl.pallas_call(
+        functools.partial(finish_kernel, count),
+        grid_spec=pltpu.PrefetchScalarGridSpec(
+            num_scalar_prefetch=1,
+            grid=grid,
+            in_specs=[step, step, whole(full_re), whole(full_im), whole(carry), whole(weave)]
+            + [pl.BlockSpec(memory_space=pl.ANY)] * len(held),
+            out_specs=[pl.BlockSpec(lead + block, lambda t, a, p: (0,) * (len(lead) + 1) + (t, a + offset, 0))]
+            * count,
+            scratch_shapes=[pltpu.VMEM((parts, *block), jnp.bfloat16)],
+        ),
+        out_shape=[jax.ShapeDtypeStruct((*lead, kl, grid[0], total * field, columns), jnp.bfloat16)] * count,
+        input_output_aliases={7: 0} if held else {},
         compiler_params=pltpu.CompilerParams(
             dimension_semantics=("arbitrary", "arbitrary"), vmem_limit_bytes=VMEM
         ),
@@ -192,7 +230,7 @@
             transcendentals=0,
         ),
         name="finish",
-    )(local_re, local_im, full_re, full_im, carry, weave)
+    )(partner, local_re, local_im, full_re, full_im, carry, weave, *held)
 
 
 def pack_kernel(green, hole, *refs):
@@ -201,46 +239,130 @@
     out[0, 1] = hole[...]
 
 
-def pack(green, hole, parts, start, wide, after):
+def pack(held, green, hole, parts, some, start, wide, after):
     kl, row_count, _, columns = green.shape
     share = row_count // parts
     steps = math.gcd(kl, 2)
     block = (kl // steps, share, wide, columns)
-    inward = pl.BlockSpec(block, lambda j, i: (i, j, start // wide, 0))
+    inward = pl.BlockSpec(block, lambda j, i: (i, j + some.start, start // wide, 0))
     shape = (parts, 2, kl, share, wide, columns)
+    extra = ([] if held is None else [held]) + list(after)
     return pl.pallas_call(
         pack_kernel,
-        grid=(parts, steps),
-        in_specs=[inward, inward] + [pl.BlockSpec(memory_space=pl.ANY)] * len(after),
-        out_specs=pl.BlockSpec((1, 2, *block), lambda j, i: (j, 0, i, 0, 0, 0)),
+        grid=(len(some), steps),
+        in_specs=[inward, inward] + [pl.BlockSpec(memory_space=pl.ANY)] * len(extra),
+        out_specs=pl.BlockSpec((1, 2, *block), lambda j, i: (j + some.start, 0, i, 0, 0, 0)),
         out_shape=jax.ShapeDtypeStruct(shape, green.dtype),
+        input_output_aliases={} if held is None else {2: 0},
         compiler_params=pltpu.CompilerParams(vmem_limit_bytes=VMEM),
-        cost_estimate=pl.CostEstimate(flops=0, bytes_accessed=4 * math.prod(shape), transcendentals=0),
+        cost_estimate=pl.CostEstimate(
+            flops=0, bytes_accessed=4 * math.prod(shape) * len(some) // parts, transcendentals=0
+        ),
         name="pack",
-    )(green, hole, *after)
+    )(green, hole, *extra)
 
 
 def place_kernel(pieces, *refs):
     refs[-1][...] = pieces[0]
 
 
-def place(result, pieces, start, shape):
+def place(result, pieces, start, field, shape):
     parts, kl, share, wide, columns = pieces.shape
     held = [] if result is None else [result]
-    steps = math.gcd(kl, 2)
-    block = (kl // steps, share, wide, columns)
+    held_wide = math.gcd(start, wide // field) * field
+    block = (kl, share, held_wide, columns)
     return pl.pallas_call(
         place_kernel,
-        grid=(parts, steps),
-        in_specs=[pl.BlockSpec((1, *block), lambda j, i: (j, i, 0, 0, 0))]
+        grid=(parts, wide // held_wide),
+        in_specs=[pl.BlockSpec((1, *block), lambda j, a: (j, 0, 0, a, 0))]
         + [pl.BlockSpec(memory_space=pl.ANY)] * len(held),
-        out_specs=pl.BlockSpec(block, lambda j, i: (i, j, start // wide, 0)),
+        out_specs=pl.BlockSpec(block, lambda j, a: (0, j, a + start * field // held_wide, 0)),
         out_shape=jax.ShapeDtypeStruct(shape, pieces.dtype),
         input_output_aliases={1: 0} if held else {},
         compiler_params=pltpu.CompilerParams(vmem_limit_bytes=VMEM),
         cost_estimate=pl.CostEstimate(flops=0, bytes_accessed=4 * math.prod(pieces.shape), transcendentals=0),
         name="place",
     )(pieces, *held)
+
+
+def pack_one_kernel(_, green, hole, *refs):
+    out = refs[-1]
+    out[0] = green[...]
+    out[1] = hole[...]
+
+
+def pack_one(green, hole, row, parts, start, wide, after):
+    kl, row_count, _, columns = green.shape
+    share = row_count // parts
+    shape = (2, kl, share, wide, columns)
+    steps = math.gcd(kl, 4)
+    block = (kl // steps, share, wide, columns)
+    inward = pl.BlockSpec(block, lambda i, row: (i, row[0], start // wide, 0))
+    return pl.pallas_call(
+        pack_one_kernel,
+        grid_spec=pltpu.PrefetchScalarGridSpec(
+            num_scalar_prefetch=1,
+            grid=(steps,),
+            in_specs=[inward, inward] + [pl.BlockSpec(memory_space=pl.ANY)] * len(after),
+            out_specs=pl.BlockSpec((2, *block), lambda i, row: (0, i, 0, 0, 0)),
+        ),
+        out_shape=jax.ShapeDtypeStruct(shape, green.dtype),
+        compiler_params=pltpu.CompilerParams(vmem_limit_bytes=VMEM),
+        cost_estimate=pl.CostEstimate(flops=0, bytes_accessed=4 * math.prod(shape), transcendentals=0),
+        name="pack_one",
+    )(row, green, hole, *after)
+
+
+def place_list_kernel(count, rows, *refs):
+    pieces, out = refs[:count], refs[-1]
+    for i, piece in enumerate(pieces):
+
+        @pl.when(pl.program_id(0) == i)
+        def _():
+            out[...] = piece[...]
+
+
+def place_list(result, pieces, rows, start, shape):
+    kl, share, wide, columns = pieces[0].shape
+    held = [] if result is None else [result]
+    count = len(pieces)
+    steps = math.gcd(kl, 1)
+    block = (kl // steps, share, wide, columns)
+
+    def inward(which):
+        return lambda i, k, rows: (jnp.where(i == which, k, jnp.where(i < which, 0, steps - 1)), 0, 0, 0)
+
+    return pl.pallas_call(
+        functools.partial(place_list_kernel, count),
+        grid_spec=pltpu.PrefetchScalarGridSpec(
+            num_scalar_prefetch=1,
+            grid=(count, steps),
+            in_specs=[pl.BlockSpec(block, inward(which)) for which in range(count)]
+            + [pl.BlockSpec(memory_space=pl.ANY)] * len(held),
+            out_specs=pl.BlockSpec(block, lambda i, k, rows: (k, rows[i], start // wide, 0)),
+        ),
+        out_shape=jax.ShapeDtypeStruct(shape, pieces[0].dtype),
+        input_output_aliases={1 + count: 0} if held else {},
+        compiler_params=pltpu.CompilerParams(vmem_limit_bytes=VMEM),
+        cost_estimate=pl.CostEstimate(
+            flops=0, bytes_accessed=4 * count * math.prod(pieces[0].shape), transcendentals=0
+        ),
+        name="place_list",
+    )(rows, *pieces, *held)
+
+
+def stack_kernel(a, b, *refs):
+    refs[-1][0] = a[...]
+    refs[-1][1] = b[...]
+
+
+def stack_after(a, b, after):
+    return pl.pallas_call(
+        stack_kernel,
+        in_specs=[pl.BlockSpec(memory_space=pltpu.VMEM)] * 2 + [pl.BlockSpec(memory_space=pl.ANY)] * len(after),
+        out_shape=jax.ShapeDtypeStruct((2, *a.shape), a.dtype),
+        name="stack_after",
+    )(a, b, *after)
 
 
 def entry(momenta, handed, site, out_part, momentum, in_part):
@@ -300,34 +422,84 @@
     field = 2 * orbitals
     share = row_count // parts
     pairs = width // field
-    sizes = [pairs // 2] * 2 if parts <= pairs else [pairs]
-    starts = [sum(sizes[:i]) * field for i in range(len(sizes))]
-
-    both = lax.all_gather(jnp.stack([decay_log, phase_step]), "mom", axis=1, tiled=True)
+    middle = pairs // 2
+    chunks = [(middle - 1, 1), (middle, middle), (0, middle - 1)] if parts <= pairs else [(0, pairs)]
+    lone = len(chunks) > 1
+
+    partners = [lax.bitwise_xor(here, jnp.int32(j)) for j in range(parts)]
+    partner = jnp.stack(partners)
+
+    def send(x, j):
+        return x if j == 0 else lax.ppermute(x, "mom", [(i, i ^ j) for i in range(parts)])
+
+    def exchange(x):
+        return lax.all_to_all(x, "mom", split_axis=0, concat_axis=0, tiled=True)
+
+    half = parts // 2
+    far, near = list(range(half, parts))[::-1], list(range(1, half))
+    mixed = [j for pair in zip(far, near + [None]) for j in pair if j]
+    gathered = [j ^ bit for j in range(half) for bit in (0, half)]
+    place_of = jnp.array([gathered.index(j) for j in range(parts)], jnp.int32)
+    positions = place_of[partner]
+
+    arrived, before, heard = [], [], []
+    for index, (start, size) in enumerate(chunks):
+        if lone and index == 0:
+            pieces = [None] * parts
+            for j in mixed + [0]:
+                piece = pack_one(green, hole, partner[j][None], parts, start * field, size * field, [])
+                pieces[j] = send(piece, j)
+            before = pieces
+        else:
+            most, rest = range(parts - 1), range(parts - 1, parts)
+            packed = pack(None, green, hole, parts, most, start * field, size * field, [])
+            if not heard:
+                after = [before[j] for j in far[:-1]] + [packed] if lone else []
+                first = stack_after(decay_log, phase_step, after)
+                both = jnp.concatenate([first, send(first, half)], axis=1)
+            after = heard[1:] if heard else before + [both]
+            packed = pack(packed, green, hole, parts, rest, start * field, size * field, after)
+            pieces = [exchange(packed)]
+            heard = heard or [send(both, j) for j in range(half)]
+        arrived.append(pieces)
+
+    both = jnp.concatenate(heard, axis=1)
     damp, turn = (x.reshape(momenta * orbitals, columns) for x in both)
     decay = jnp.exp(damp)
-    step_re, step_im, tile_re, tile_im, full_re, full_im = prepare(decay * jnp.cos(turn), decay * jnp.sin(turn))
+    step_re, step_im, tile_re, tile_im, full_re, full_im = prepare(
+        positions, decay * jnp.cos(turn), decay * jnp.sin(turn)
+    )
     totals = lax.all_gather(jnp.stack([full_re[:, -1], full_im[:, -1]]), "tm")
     tables = transform_tables(momenta, orbitals, jnp.arange(momenta, dtype=jnp.int32))
     group = min(momenta, 8) * orbitals
     weave = weave_table(group)
 
-    def exchange(x):
-        return lax.all_to_all(x, "mom", split_axis=0, concat_axis=0, tiled=True)
-
-    arrived = [
-        exchange(pack(green, hole, parts, start, size * field, [both] if start == 0 else []))
-        for start, size in zip(starts, sizes)
-    ]
-    result, after = None, []
-    for pieces, start, size in zip(arrived, starts, sizes):
-        local_re, local_im, ends = local_history(pieces, tables, (step_re, step_im, tile_re, tile_im), after)
+    result, finished, after = None, None, []
+    for index, (pieces, (start, size)) in enumerate(zip(arrived, chunks)):
+        local_re, local_im, ends = local_history(
+            pieces, partner, tables, (step_re, step_im, tile_re, tile_im), after
+        )
         number = share * size
         enter = carries("tm", ends[:, :, :number], totals[:, 0], totals[:, 1])
         enter = jnp.pad(enter, ((0, 0), (0, 0), (0, LANES - number)))
-        pieces = finish(parts, momenta, local_re, local_im, full_re, full_im, enter, weave, (share, size))
-        after = [pieces]
-        result = place(result, exchange(pieces), start, green.shape)
+        joined = lone and index < 2
+        first = chunks[0][0] if joined else start
+        total = chunks[0][1] + chunks[1][1] if joined else size
+        split = lone and index == 2
+        outs = finish(
+            finished if joined else None, start - first, total, partner, split, momenta,
+            local_re, local_im, full_re, full_im, enter, weave, (share, size),
+        )
+        finished = outs[0]
+        after = [finished]
+        if split:
+            order = [0] + near[1:] + far[:1] + near[:1] + far[1:]
+            for some in order[:-3], order[-3:-1], order[-1:]:
+                moved = [send(outs[j], j) for j in some]
+                rows = jnp.stack([partner[j] for j in some])
+                result = place_list(result, moved, rows, start * field, green.shape)
+        elif not (lone and index == 0):
+            result = place(result, exchange(finished), first, field, green.shape)
     return result
 
 

time: 1200 us -> 1150 us (0.958)
  waiting for transfers between devices: 821 us -> 622 us
  starting transfers between devices: 21.6 us -> 111 us
  Pallas kernels: 275 us -> 325 us
  between operations: 13.6 us -> 0.39 us
    all_to_all x4 -> x3, waiting for transfers between devices: 776 us -> 212 us  [exchange(): return lax.all_to_all(x, 'mom', split_axis=0, concat_axis=0, tiled=True)]
    ppermute x0 -> x18, waiting for transfers between devices: none -> 410 us  [send(): lax.ppermute(x, 'mom', [(i, i ^ j) for i in range(parts)])]
    ppermute x0 -> x18, starting transfers between devices: none -> 90.3 us  [send(): lax.ppermute(x, 'mom', [(i, i ^ j) for i in range(parts)])]
    pallas_call x9 -> x24, Pallas kernels: 275 us -> 325 us  [the longest x3 181 us: local_history(): pl.pallas_call(functools.partial(local_kernel, len(pieces)), grid_spec=pl...]
    all_gather x1 -> x0, waiting for transfers between devices: 44.4 us -> none  [shards(): lax.all_gather(jnp.stack([decay_log, phase_step]), 'mom', axis=1, tiled=T...]
  transfers between devices with their start and end apart: 5 -> 21, of which waited for: 5 -> 12; matrix products, arithmetic and copies ran while one was open for 4% -> 5% of each run, Pallas kernels for 21% -> 28%
where the time goes in v2:
time: 1150 us; the launch traced here: 1140 us
  waiting for transfers between devices  622 us (54%)
  Pallas kernels  325 us (28%)
  starting transfers between devices  111 us (10%)
  other arithmetic  44.1 us (4%)
  blocking collectives  22.6 us (2%)
  local copies, waits for them, and re-layouts  12.5 us (1%)
    ppermute x18, waiting for transfers between devices, send(): lax.ppermute(x, 'mom', [(i, i ^ j) for i in range(parts)])  410 us
    all_to_all x3, waiting for transfers between devices, exchange(): return lax.all_to_all(x, 'mom', split_axis=0, concat_axis=0, tiled=True)  212 us
    pallas_call x3, Pallas kernels, local_history(): pl.pallas_call(functools.partial(local_kernel, len(pieces)), grid_spec=pl...  181 us
    ppermute x18, starting transfers between devices, send(): lax.ppermute(x, 'mom', [(i, i ^ j) for i in range(parts)])  90.3 us
    select_n x1, other arithmetic, table(): return jnp.where(b == d, value, jnp.zeros_like(value))  38.8 us
    pallas_call x3, Pallas kernels, finish(): pl.pallas_call(functools.partial(finish_kernel, count), grid_spec=pltpu.P...  38.2 us
    pallas_call x4, Pallas kernels, pack(): pl.pallas_call(pack_kernel, grid=(len(some), steps), in_specs=[inward, in...  33.4 us
    pallas_call x8, Pallas kernels, pack_one(): pl.pallas_call(pack_one_kernel, grid_spec=pltpu.PrefetchScalarGridSpec(nu...  24.6 us
  transfers between devices with their start and end apart: 21, of which 12 were waited for; matrix products, arithmetic and copies ran while one was open for 5% of the time, Pallas kernels for 28%

profile of v2, /device:TPU:0, one launch (start us, length us, event | category | flops | bytes accessed | tf_op | source)
XLA Modules:
  0.0 1136.8 jit_solution(4826304095103277199)
XLA Ops:
  32.1 34.7 %collective-permute-start.8 = (bf16[2,8,4,16,256]{4,3,2,1,0:T(8,128)(2,1)}, bf16[2,8,4,16,256]{4,3,2,1,0:T(8,128)(2,1)S(1)}, u32[]{:S(2)}, u32[]{:S(2)}) collective-permute-start(bf16[2,8,4,16,256]{4,3,2,1,0:T(8,128)(2,1)} %pack_one.13), channel_id=1, source_target_pairs={{0,8},{4,12},{8,0},{12,4},{16,24},{20,28},{24,16},{28,20},{1,9},{5... | collective-permute-start | bytes 1572872 | tf_op jit(solution)/shard_map/ppermute | solution.py:433
  66.9 11.2 collective-permute-start.9
  78.1 15.2 %pack.5.refs_3_.refs_0_ = bf16[8,2,8,4,64,256]{5,4,3,2,1,0:T(8,128)(2,1)} custom-call(bf16[8,32,128,256]{3,2,1,0:T(8,128)(2,1)} %green.23, bf16[8,32,128,256]{3,2,1,0:T(8,128)(2,1)} %hole.23), custom_call_target="tpu_custom_call" | custom-call | bytes 29360128 | tf_op jit(solution)/shard_map/pack/pallas_call | solution.py:250
  105.6 9.3 collective-permute-done.9.refs_4_.refs_3_
  127.0 13.2 %pack.4.refs_0_ = bf16[8,2,8,4,48,256]{5,4,3,2,1,0:T(8,128)(2,1)} custom-call(bf16[8,32,128,256]{3,2,1,0:T(8,128)(2,1)} %green.23, bf16[8,32,128,256]{3,2,1,0:T(8,128)(2,1)} %hole.23), custom_call_target="tpu_custom_call" | custom-call | bytes 22020096 | tf_op jit(solution)/shard_map/pack/pallas_call | solution.py:250
  140.2 124.4 %collective-permute-done.4.refs_1_ = f32[2,16,8,256]{3,2,1,0:T(8,128)S(1)} collective-permute-done((f32[2,16,8,256]{3,2,1,0:T(8,128)S(1)}, f32[2,16,8,256]{3,2,1,0:T(8,128)S(1)}, u32[]{:S(2)}, u32[]{:S(2)}) %collective-permute-start.4) | collective-permute-done | bytes 262176 | tf_op jit(solution)/shard_map/ppermute | solution.py:433
  264.7 136.0 %collective-permute-done.5.refs_2_ = f32[2,16,8,256]{3,2,1,0:T(8,128)S(1)} collective-permute-done((f32[2,16,8,256]{3,2,1,0:T(8,128)S(1)}, f32[2,16,8,256]{3,2,1,0:T(8,128)S(1)}, u32[]{:S(2)}, u32[]{:S(2)}) %collective-permute-start.5) | collective-permute-done | bytes 262176 | tf_op jit(solution)/shard_map/ppermute | solution.py:433
  407.0 78.0 %all-to-all-done.1.refs_0_ = bf16[8,2,8,4,64,256]{5,4,3,2,1,0:T(8,128)(2,1)} async-done(((bf16[8,2,8,4,64,256]{5,4,3,2,1,0:T(8,128)(2,1)}), bf16[8,2,8,4,64,256]{5,4,3,2,1,0:T(8,128)(2,1)}, u32[]{:S(2)}, u32[]{:S(2)}) %all-to-all-start.1) | async-done | bytes 16777248 | tf_op jit(solution)/shard_map/all_to_all | solution.py:436
  485.0 9.2 all-to-all-start
  497.1 38.8 %compare_select_fusion.2 = (bf16[1024,1024]{1,0:T(8,128)(2,1)}, bf16[1024,1024]{1,0:T(8,128)(2,1)}, bf16[1024,1024]{1,0:T(8,128)(2,1)}) fusion(s32[1024]{0:T(1024)S(1)} %mul.645, s32[1024]{0:T(1024)S(1)} %get-tuple-element.78, s32[1024]{0:T(1024)S(1)} %get-tuple-element.77, s32[1024]{0:T(1024)S(1)} %get-tuple-element.80, s32[1024]{0:T(1024)S(1)} %get-tuple-element.79, ...), kind=kLoop, calls=%fused_computation.13 | loop fusion | flops 62914560 | bytes 6321152 | tf_op jit(solution)/shard_map/jit(_where)/select_n | solution.py:390
  538.8 10.9 prepare.1
  549.7 27.7 %local_history.3 = (f32[4,512,256]{2,1,0:T(8,128)}, f32[4,512,256]{2,1,0:T(8,128)}, f32[2,512,128]{2,1,0:T(8,128)}) custom-call(s32[8]{0:T(128)} %stack.77.partner, bf16[2,8,4,16,256]{4,3,2,1,0:T(8,128)(2,1)} %pack_one.11.refs_1_.refs_0_, bf16[2,8,4,16,256]{4,3,2,1,0:T(8,128)(2,1)} %copy-done.19, bf16[2,8,4,16,256]{4,3,2,1,0:T(8,128)(2,1)} %copy-done.20, ...), custom_call_target="tpu_custom_call" | custom-call | flops 32212254720 | bytes 8388608 | tf_op jit(solution)/shard_map/local_history/pallas_call | solution.py:139
  590.9 6.1 finish.3.refs_8_.refs_0_
  597.0 86.8 %local_history.4 = (f32[16,512,256]{2,1,0:T(8,128)}, f32[16,512,256]{2,1,0:T(8,128)}, f32[2,512,128]{2,1,0:T(8,128)}) custom-call(s32[8]{0:T(128)} %stack.77.partner, bf16[8,2,8,4,64,256]{5,4,3,2,1,0:T(8,128)(2,1)} %all-to-all-done.1.refs_0_, bf16[1024,1024]{1,0:T(8,128)(2,1)} %get-tuple-element.69.refs_8_.refs_1_, ...), custom_call_target="tpu_custom_call" | custom-call | flops 128849018880 | bytes 33554432 | tf_op jit(solution)/shard_map/local_history/pallas_call | solution.py:139
  692.1 17.8 %finish.4.refs_8_ = bf16[8,8,4,80,256]{4,3,2,1,0:T(8,128)(2,1)} custom-call(s32[8]{0:T(128)} %stack.77.partner, f32[16,512,256]{2,1,0:T(8,128)} %get-tuple-element.37.re_ref, f32[16,512,256]{2,1,0:T(8,128)} %get-tuple-element.38.im_ref, f32[512,256]{1,0:T(8,128)} %get-tuple-element.34.full_re, ...), custom_call_target="tpu_custom_call", output_to_operand_aliasing={{}: (7, {})} | custom-call | flops 20971520 | bytes 62914560 | tf_op jit(solution)/shard_map/finish/pallas_call | solution.py:211
  709.9 57.5 %all-to-all-done.refs_0_ = bf16[8,2,8,4,48,256]{5,4,3,2,1,0:T(8,128)(2,1)} async-done(((bf16[8,2,8,4,48,256]{5,4,3,2,1,0:T(8,128)(2,1)}), bf16[8,2,8,4,48,256]{5,4,3,2,1,0:T(8,128)(2,1)}, u32[]{:S(2)}, u32[]{:S(2)}) %all-to-all-start) | async-done | bytes 12582944 | tf_op jit(solution)/shard_map/all_to_all | solution.py:436
  772.6 66.8 %local_history.5 = (f32[12,512,256]{2,1,0:T(8,128)}, f32[12,512,256]{2,1,0:T(8,128)}, f32[2,512,128]{2,1,0:T(8,128)}) custom-call(s32[8]{0:T(128)} %stack.77.partner, bf16[8,2,8,4,48,256]{5,4,3,2,1,0:T(8,128)(2,1)} %all-to-all-done.refs_0_, bf16[1024,1024]{1,0:T(8,128)(2,1)} %get-tuple-element.69.refs_8_.refs_1_, ...), custom_call_target="tpu_custom_call" | custom-call | flops 96636764160 | bytes 25165824 | tf_op jit(solution)/shard_map/local_history/pallas_call | solution.py:139
  848.1 14.2 %finish.5 = (bf16[8,4,48,256]{3,2,1,0:T(8,128)(2,1)}, bf16[8,4,48,256]{3,2,1,0:T(8,128)(2,1)}, bf16[8,4,48,256]{3,2,1,0:T(8,128)(2,1)}, bf16[8,4,48,256]{3,2,1,0...) custom-call(s32[8]{0:T(128)} %stack.77.partner, ...), custom_call_target="tpu_custom_call" | custom-call | flops 15728640 | bytes 47185920 | tf_op jit(solution)/shard_map/finish/pallas_call | solution.py:211
  871.1 89.1 %collective-permute-done.14.refs_1_ = bf16[8,4,48,256]{3,2,1,0:T(8,128)(2,1)S(1)} collective-permute-done((bf16[8,4,48,256]{3,2,1,0:T(8,128)(2,1)}, bf16[8,4,48,256]{3,2,1,0:T(8,128)(2,1)S(1)}, u32[]{:S(2)}, u32[]{:S(2)}) %collective-permute-start.14) | collective-permute-done | bytes 786464 | tf_op jit(solution)/shard_map/ppermute | solution.py:433
  965.1 11.8 %collective-permute-done.15.refs_2_ = bf16[8,4,48,256]{3,2,1,0:T(8,128)(2,1)S(1)} collective-permute-done((bf16[8,4,48,256]{3,2,1,0:T(8,128)(2,1)}, bf16[8,4,48,256]{3,2,1,0:T(8,128)(2,1)S(1)}, u32[]{:S(2)}, u32[]{:S(2)}) %collective-permute-start.15) | collective-permute-done | bytes 786464 | tf_op jit(solution)/shard_map/ppermute | solution.py:433
  977.0 15.1 %collective-permute-start.11 = (bf16[8,4,48,256]{3,2,1,0:T(8,128)(2,1)}, bf16[8,4,48,256]{3,2,1,0:T(8,128)(2,1)}, u32[]{:S(2)}, u32[]{:S(2)}) collective-permute-start(bf16[8,4,48,256]{3,2,1,0:T(8,128)(2,1)} %get-tuple-element.43), channel_id=1, source_target_pairs={{0,16},{4,20},{8,24},{12,28},{16,0},{20,4},{24,8},{28,12},{1,17},{... | collective-permute-start | bytes 2359304 | tf_op jit(solution)/shard_map/ppermute | solution.py:433
  993.4 76.1 %all-to-all-done.2.pieces = bf16[8,8,4,80,256]{4,3,2,1,0:T(8,128)(2,1)} async-done(((bf16[8,8,4,80,256]{4,3,2,1,0:T(8,128)(2,1)}), bf16[8,8,4,80,256]{4,3,2,1,0:T(8,128)(2,1)}, u32[]{:S(2)}, u32[]{:S(2)}) %all-to-all-start.2) | async-done | bytes 10485792 | tf_op jit(solution)/shard_map/all_to_all | solution.py:436
  1069.5 23.7 %place.1.refs_5_ = bf16[8,32,128,256]{3,2,1,0:T(8,128)(2,1)} custom-call(bf16[8,8,4,80,256]{4,3,2,1,0:T(8,128)(2,1)} %all-to-all-done.2.pieces), custom_call_target="tpu_custom_call" | custom-call | bytes 20971520 | tf_op jit(solution)/shard_map/place/pallas_call | solution.py:274
  1099.7 31.0 %collective-permute-done.13.refs_1_ = bf16[8,4,48,256]{3,2,1,0:T(8,128)(2,1)} collective-permute-done((bf16[8,4,48,256]{3,2,1,0:T(8,128)(2,1)}, bf16[8,4,48,256]{3,2,1,0:T(8,128)(2,1)}, u32[]{:S(2)}, u32[]{:S(2)}) %collective-permute-start.13) | collective-permute-done | bytes 786464 | tf_op jit(solution)/shard_map/ppermute | solution.py:433
  (142 shorter events, 131.5 us)
Async XLA Ops:
  3.1 29.0 %collective-permute-start = (bf16[2,8,4,16,256]{4,3,2,1,0:T(8,128)(2,1)}, bf16[2,8,4,16,256]{4,3,2,1,0:T(8,128)(2,1)S(1)}, u32[]{:S(2)}, u32[]{:S(2)}) collective-permute-start(bf16[2,8,4,16,256]{4,3,2,1,0:T(8,128)(2,1)} %pack_one.8), channel_id=1, source_target_pairs={{0,28},{4,24},{8,20},{12,16},{16,12},{20,8},{24,4},{28,0},{1,29},{... | collective-permute-start | bytes 1572872 | tf_op jit(solution)/shard_map/ppermute | solution.py:433
  12.1 54.7 %collective-permute-start.1 = (bf16[2,8,4,16,256]{4,3,2,1,0:T(8,128)(2,1)}, bf16[2,8,4,16,256]{4,3,2,1,0:T(8,128)(2,1)S(1)}, u32[]{:S(2)}, u32[]{:S(2)}) collective-permute-start(bf16[2,8,4,16,256]{4,3,2,1,0:T(8,128)(2,1)} %pack_one.9), channel_id=1, source_target_pairs={{0,24},{4,28},{8,16},{12,20},{16,8},{20,12},{24,0},{28,4},{1,25},{... | collective-permute-start | bytes 1572872 | tf_op jit(solution)/shard_map/ppermute | solution.py:433
  15.4 77.8 %collective-permute-start.2 = (bf16[2,8,4,16,256]{4,3,2,1,0:T(8,128)(2,1)}, bf16[2,8,4,16,256]{4,3,2,1,0:T(8,128)(2,1)S(1)}, u32[]{:S(2)}, u32[]{:S(2)}) collective-permute-start(bf16[2,8,4,16,256]{4,3,2,1,0:T(8,128)(2,1)} %pack_one.10), channel_id=1, source_target_pairs={{0,20},{4,16},{8,28},{12,24},{16,4},{20,0},{24,12},{28,8},{1,21},{... | collective-permute-start | bytes 1572872 | tf_op jit(solution)/shard_map/ppermute | solution.py:433
  19.3 86.3 %collective-permute-start.10 = (bf16[2,8,4,16,256]{4,3,2,1,0:T(8,128)(2,1)}, bf16[2,8,4,16,256]{4,3,2,1,0:T(8,128)(2,1)S(1)}, u32[]{:S(2)}, u32[]{:S(2)}) collective-permute-start(bf16[2,8,4,16,256]{4,3,2,1,0:T(8,128)(2,1)} %pack_one.15), channel_id=1, source_target_pairs={{0,16},{4,20},{8,24},{12,28},{16,0},{20,4},{24,8},{28,12},{1,17},{... | collective-permute-start | bytes 1572872 | tf_op jit(solution)/shard_map/ppermute | solution.py:433
  24.3 81.3 %collective-permute-start.7 = (bf16[2,8,4,16,256]{4,3,2,1,0:T(8,128)(2,1)}, bf16[2,8,4,16,256]{4,3,2,1,0:T(8,128)(2,1)S(1)}, u32[]{:S(2)}, u32[]{:S(2)}) collective-permute-start(bf16[2,8,4,16,256]{4,3,2,1,0:T(8,128)(2,1)} %pack_one.12), channel_id=1, source_target_pairs={{0,4},{4,0},{8,12},{12,8},{16,20},{20,16},{24,28},{28,24},{1,5},{5... | collective-permute-start | bytes 1572872 | tf_op jit(solution)/shard_map/ppermute | solution.py:433
  32.1 73.5 %collective-permute-start.8 = (bf16[2,8,4,16,256]{4,3,2,1,0:T(8,128)(2,1)}, bf16[2,8,4,16,256]{4,3,2,1,0:T(8,128)(2,1)S(1)}, u32[]{:S(2)}, u32[]{:S(2)}) collective-permute-start(bf16[2,8,4,16,256]{4,3,2,1,0:T(8,128)(2,1)} %pack_one.13), channel_id=1, source_target_pairs={{0,8},{4,12},{8,0},{12,4},{16,24},{20,28},{24,16},{28,20},{1,9},{5... | collective-permute-start | bytes 1572872 | tf_op jit(solution)/shard_map/ppermute | solution.py:433
  66.9 48.1 %collective-permute-start.9 = (bf16[2,8,4,16,256]{4,3,2,1,0:T(8,128)(2,1)}, bf16[2,8,4,16,256]{4,3,2,1,0:T(8,128)(2,1)}, u32[]{:S(2)}, u32[]{:S(2)}) collective-permute-start(bf16[2,8,4,16,256]{4,3,2,1,0:T(8,128)(2,1)} %pack_one.14), channel_id=1, source_target_pairs={{0,12},{4,8},{8,4},{12,0},{16,28},{20,24},{24,20},{28,16},{1,13},{... | collective-permute-start | bytes 1572872 | tf_op jit(solution)/shard_map/ppermute | solution.py:433
  95.6 9.2 collective-permute-start.3
  117.6 367.5 %all-to-all-start.1 = ((bf16[8,2,8,4,64,256]{5,4,3,2,1,0:T(8,128)(2,1)}), bf16[8,2,8,4,64,256]{5,4,3,2,1,0:T(8,128)(2,1)}, u32[]{:S(2)}, u32[]{:S(2)}) async-start(bf16[8,2,8,4,64,256]{5,4,3,2,1,0:T(8,128)(2,1)} %pack.7), calls=%async_computation.1 | async-start | bytes 33554432 | tf_op jit(solution)/shard_map/all_to_all | solution.py:436
  123.5 141.2 %collective-permute-start.4 = (f32[2,16,8,256]{3,2,1,0:T(8,128)S(1)}, f32[2,16,8,256]{3,2,1,0:T(8,128)S(1)}, u32[]{:S(2)}, u32[]{:S(2)}) collective-permute-start(f32[2,16,8,256]{3,2,1,0:T(8,128)S(1)} %copy-done.13), channel_id=1, source_target_pairs={{0,4},{4,0},{8,12},{12,8},{16,20},{20,16},{24,28},{28,24},{1,5},{5... | collective-permute-start | bytes 786440 | tf_op jit(solution)/shard_map/ppermute | solution.py:433
  125.3 275.3 %collective-permute-start.5 = (f32[2,16,8,256]{3,2,1,0:T(8,128)S(1)}, f32[2,16,8,256]{3,2,1,0:T(8,128)S(1)}, u32[]{:S(2)}, u32[]{:S(2)}) collective-permute-start(f32[2,16,8,256]{3,2,1,0:T(8,128)S(1)} %copy-done.13), channel_id=1, source_target_pairs={{0,8},{4,12},{8,0},{12,4},{16,24},{20,28},{24,16},{28,20},{1,9},{5... | collective-permute-start | bytes 786440 | tf_op jit(solution)/shard_map/ppermute | solution.py:433
  126.8 277.1 %collective-permute-start.6 = (f32[2,16,8,256]{3,2,1,0:T(8,128)S(1)}, f32[2,16,8,256]{3,2,1,0:T(8,128)S(1)}, u32[]{:S(2)}, u32[]{:S(2)}) collective-permute-start(f32[2,16,8,256]{3,2,1,0:T(8,128)S(1)} %copy-done.13), channel_id=1, source_target_pairs={{0,12},{4,8},{8,4},{12,0},{16,28},{20,24},{24,20},{28,16},{1,13},{... | collective-permute-start | bytes 786440 | tf_op jit(solution)/shard_map/ppermute | solution.py:433
  264.6 139.2 %copy-start.7 = (f32[2,16,8,256]{3,2,1,0:T(8,128)}, f32[2,16,8,256]{3,2,1,0:T(8,128)S(1)}, u32[]{:S(2)}) copy-start(f32[2,16,8,256]{3,2,1,0:T(8,128)S(1)} %collective-permute-done.4.refs_1_) | copy-start | bytes 786436
  485.0 282.4 %all-to-all-start = ((bf16[8,2,8,4,48,256]{5,4,3,2,1,0:T(8,128)(2,1)}), bf16[8,2,8,4,48,256]{5,4,3,2,1,0:T(8,128)(2,1)}, u32[]{:S(2)}, u32[]{:S(2)}) async-start(bf16[8,2,8,4,48,256]{5,4,3,2,1,0:T(8,128)(2,1)} %pack.6), calls=%async_computation | async-start | bytes 25165824 | tf_op jit(solution)/shard_map/all_to_all | solution.py:436
  767.4 302.0 %all-to-all-start.2 = ((bf16[8,8,4,80,256]{4,3,2,1,0:T(8,128)(2,1)}), bf16[8,8,4,80,256]{4,3,2,1,0:T(8,128)(2,1)}, u32[]{:S(2)}, u32[]{:S(2)}) async-start(bf16[8,8,4,80,256]{4,3,2,1,0:T(8,128)(2,1)} %finish.4.refs_8_), calls=%async_computation.2 | async-start | bytes 20971520 | tf_op jit(solution)/shard_map/all_to_all | solution.py:436
  862.4 97.8 %collective-permute-start.14 = (bf16[8,4,48,256]{3,2,1,0:T(8,128)(2,1)}, bf16[8,4,48,256]{3,2,1,0:T(8,128)(2,1)S(1)}, u32[]{:S(2)}, u32[]{:S(2)}) collective-permute-start(bf16[8,4,48,256]{3,2,1,0:T(8,128)(2,1)} %get-tuple-element.47), channel_id=1, source_target_pairs={{0,8},{4,12},{8,0},{12,4},{16,24},{20,28},{24,16},{28,20},{1,9},{5... | collective-permute-start | bytes 2359304 | tf_op jit(solution)/shard_map/ppermute | solution.py:433
  864.3 112.6 %collective-permute-start.15 = (bf16[8,4,48,256]{3,2,1,0:T(8,128)(2,1)}, bf16[8,4,48,256]{3,2,1,0:T(8,128)(2,1)S(1)}, u32[]{:S(2)}, u32[]{:S(2)}) collective-permute-start(bf16[8,4,48,256]{3,2,1,0:T(8,128)(2,1)} %get-tuple-element.48), channel_id=1, source_target_pairs={{0,12},{4,8},{8,4},{12,0},{16,28},{20,24},{24,20},{28,16},{1,13},{... | collective-permute-start | bytes 2359304 | tf_op jit(solution)/shard_map/ppermute | solution.py:433
  865.8 227.4 %collective-permute-start.16 = (bf16[8,4,48,256]{3,2,1,0:T(8,128)(2,1)}, bf16[8,4,48,256]{3,2,1,0:T(8,128)(2,1)S(1)}, u32[]{:S(2)}, u32[]{:S(2)}) collective-permute-start(bf16[8,4,48,256]{3,2,1,0:T(8,128)(2,1)} %get-tuple-element.49), channel_id=1, source_target_pairs={{0,28},{4,24},{8,20},{12,16},{16,12},{20,8},{24,4},{28,0},{1,29},{... | collective-permute-start | bytes 2359304 | tf_op jit(solution)/shard_map/ppermute | solution.py:433
  869.1 224.1 %collective-permute-start.17 = (bf16[8,4,48,256]{3,2,1,0:T(8,128)(2,1)}, bf16[8,4,48,256]{3,2,1,0:T(8,128)(2,1)}, u32[]{:S(2)}, u32[]{:S(2)}) collective-permute-start(bf16[8,4,48,256]{3,2,1,0:T(8,128)(2,1)} %get-tuple-element.50), channel_id=1, source_target_pairs={{0,4},{4,0},{8,12},{12,8},{16,20},{20,16},{24,28},{28,24},{1,5},{5... | collective-permute-start | bytes 2359304 | tf_op jit(solution)/shard_map/ppermute | solution.py:433
  870.6 229.1 %collective-permute-start.12 = (bf16[8,4,48,256]{3,2,1,0:T(8,128)(2,1)}, bf16[8,4,48,256]{3,2,1,0:T(8,128)(2,1)S(1)}, u32[]{:S(2)}, u32[]{:S(2)}) collective-permute-start(bf16[8,4,48,256]{3,2,1,0:T(8,128)(2,1)} %get-tuple-element.44), channel_id=1, source_target_pairs={{0,24},{4,28},{8,16},{12,20},{16,8},{20,12},{24,0},{28,4},{1,25},{... | collective-permute-start | bytes 2359304 | tf_op jit(solution)/shard_map/ppermute | solution.py:433
  960.1 133.0 %copy-start.14 = (bf16[8,4,48,256]{3,2,1,0:T(8,128)(2,1)}, bf16[8,4,48,256]{3,2,1,0:T(8,128)(2,1)S(1)}, u32[]{:S(2)}) copy-start(bf16[8,4,48,256]{3,2,1,0:T(8,128)(2,1)S(1)} %collective-permute-done.14.refs_1_) | copy-start | bytes 2359300
  960.1 170.6 %collective-permute-start.13 = (bf16[8,4,48,256]{3,2,1,0:T(8,128)(2,1)}, bf16[8,4,48,256]{3,2,1,0:T(8,128)(2,1)}, u32[]{:S(2)}, u32[]{:S(2)}) collective-permute-start(bf16[8,4,48,256]{3,2,1,0:T(8,128)(2,1)} %get-tuple-element.45), channel_id=1, source_target_pairs={{0,20},{4,16},{8,28},{12,24},{16,4},{20,0},{24,12},{28,8},{1,21},{... | collective-permute-start | bytes 2359304 | tf_op jit(solution)/shard_map/ppermute | solution.py:433
  977.0 116.2 %copy-start.16 = (bf16[8,4,48,256]{3,2,1,0:T(8,128)(2,1)}, bf16[8,4,48,256]{3,2,1,0:T(8,128)(2,1)S(1)}, u32[]{:S(2)}) copy-start(bf16[8,4,48,256]{3,2,1,0:T(8,128)(2,1)S(1)} %collective-permute-done.15.refs_2_) | copy-start | bytes 2359300
  977.0 157.8 %collective-permute-start.11 = (bf16[8,4,48,256]{3,2,1,0:T(8,128)(2,1)}, bf16[8,4,48,256]{3,2,1,0:T(8,128)(2,1)}, u32[]{:S(2)}, u32[]{:S(2)}) collective-permute-start(bf16[8,4,48,256]{3,2,1,0:T(8,128)(2,1)} %get-tuple-element.43), channel_id=1, source_target_pairs={{0,16},{4,20},{8,24},{12,28},{16,0},{20,4},{24,8},{28,12},{1,17},{... | collective-permute-start | bytes 2359304 | tf_op jit(solution)/shard_map/ppermute | solution.py:433
  (18 other events, 428.8 us)
